TPU v7x, 32 devices: a whole 2x2x4 slice. The times are simulated.
32 devices in a mesh: band: 2 (over x), gx: 16 (over z, y, core).
Axes of the slice: x: 2, y: 2, z: 4, core: 2. Of those that a mesh axis runs over, the one named last changes fastest.
Arguments:
- slc_tiles: bfloat16 [64, 2, 64, 2048], P('gx', None, 'band'), parts along dimension 2, may hold values from -64 to 64
- look_weight: float32 [64, 2048], P('band'), parts along dimension 0, may hold values from 0.05 to 1
- pair_list: int32 [192, 2], replicated, may hold values from 0 to 63, as said below
Outputs:
- corrected: float32 [64, 64, 2048], P(None, 'band', 'gx'), parts along dimension 1
There are 2 independent parts, one for each index of `band`. A program takes and returns all parts, laid end to end along the dimension named above; an argument that names none is the same for every part. Nothing has to cross between parts.
Inputs may be any that keep to these rules, and one draw needn't show every extreme that they name: `pair_list`: row p is a pair of date indices; with d = p // 12, the reference date lies in d * 4 to (d + 1) * 4 - 1 and the secondary date is 1 to 4 dates after it.
All inputs are finite; a program needn't handle non-finite values.
Results may differ from a plain program's by a relative error of at most 0.0071.
Values may be sent and summed in bfloat16 or wider, within the bound.
A program may use at most 128 MiB of HBM per device.

v0:
```python
import jax
import jax.numpy as jnp
from jax import lax
from jax.sharding import PartitionSpec as P

LOOK = 9


def from_behind(block, axis, distance):
    devices = range(lax.axis_size(axis))
    route = [(i - distance, i) for i in devices if i - distance in devices]
    return lax.ppermute(block, axis, route)


def box_sum(values, col_count):
    rim_width = LOOK // 2
    row_count = values.shape[-2]
    padded = jnp.pad(values, [(0, 0)] * (values.ndim - 2) + [(rim_width, rim_width), (0, 0)])
    running = padded[..., 0:row_count, :]
    for offset in range(1, LOOK):
        running = running + padded[..., offset : offset + row_count, :]
    summed = running[..., 0:col_count]
    for offset in range(1, LOOK):
        summed = summed + running[..., offset : offset + col_count]
    return summed


def observe(first_tile, second_tile, weight, col_count):
    first_re = first_tile[..., 0, :, :].astype(jnp.float32)
    first_im = first_tile[..., 1, :, :].astype(jnp.float32)
    second_re = second_tile[..., 0, :, :].astype(jnp.float32)
    second_im = second_tile[..., 1, :, :].astype(jnp.float32)
    cross_re = weight * (first_re * second_re + first_im * second_im)
    cross_im = weight * (first_im * second_re - first_re * second_im)
    power_first = weight * (first_re * first_re + first_im * first_im)
    power_second = weight * (second_re * second_re + second_im * second_im)
    stacked = jnp.stack([cross_re, cross_im, power_first, power_second], axis=0)
    looked = box_sum(stacked, col_count)
    return (looked[1] * lax.rsqrt(looked[2] * looked[3] + 1e-06)).astype(jnp.bfloat16)


def solve_normal(normal_matrix, projected):
    factor = jnp.linalg.cholesky(normal_matrix)
    return jax.scipy.linalg.cho_solve((factor, True), projected)


def body(slc_tiles, look_weight, pair_list):
    rim_width = LOOK // 2
    devices = lax.axis_size("gx")
    position = lax.axis_index("gx")
    date_dev = slc_tiles.shape[0]
    row_count = slc_tiles.shape[2]
    col_total = slc_tiles.shape[3]
    strip_cols = col_total // devices
    pair_total = pair_list.shape[0]
    pair_dev = pair_total // devices
    date_total = date_dev * devices
    weight_pad = jnp.pad(look_weight, ((0, 0), (rim_width, rim_width)))
    following = from_behind(slc_tiles, "gx", -1)
    local_tiles = jnp.concatenate([slc_tiles, following], axis=0)
    local_tiles = jnp.pad(local_tiles, ((0, 0), (0, 0), (0, 0), (rim_width, rim_width)))
    own_pairs = (
        lax.dynamic_slice_in_dim(pair_list, position * pair_dev, pair_dev, 0) - position * date_dev
    )

    def one_pair(pair_row):
        return observe(local_tiles[pair_row[0]], local_tiles[pair_row[1]], weight_pad, col_total)

    observed = lax.map(one_pair, own_pairs)
    blocks = observed.reshape(pair_dev, row_count, devices, strip_cols)
    strips = lax.all_to_all(blocks, "gx", split_axis=2, concat_axis=0, tiled=True)
    strips = strips.reshape(pair_total, row_count * strip_cols)
    date_ids = lax.iota(jnp.int32, date_total)
    incidence = (
        (date_ids[:, None] == pair_list[None, :, 0]).astype(jnp.float32)
        - (date_ids[:, None] == pair_list[None, :, 1]).astype(jnp.float32)
    ).astype(jnp.bfloat16)
    normal_matrix = jnp.dot(incidence, incidence.T, preferred_element_type=jnp.float32) + jnp.eye(
        date_total, dtype=jnp.float32
    )
    projected = jnp.dot(incidence, strips, preferred_element_type=jnp.float32)
    series = solve_normal(normal_matrix, projected).reshape(date_total, row_count, strip_cols)
    column_ids = position * strip_cols + lax.iota(jnp.int32, strip_cols)
    columns = (2.0 * column_ids.astype(jnp.float32) + 1.0) / col_total - 1.0
    all_cols = (2.0 * lax.iota(jnp.int32, col_total).astype(jnp.float32) + 1.0) / col_total - 1.0
    square_sum = jnp.sum(all_cols * all_cols)
    partial_mean = jnp.sum(series, axis=(1, 2))
    partial_slope = jnp.sum(series * columns, axis=(1, 2))
    totals = lax.psum((partial_mean, partial_slope), "gx")
    date_mean = totals[0] / (row_count * col_total)
    date_slope = totals[1] / (row_count * square_sum)
    return series - date_mean[:, None, None] - date_slope[:, None, None] * columns


def solution(mesh):
    return jax.shard_map(
        body,
        mesh=mesh,
        in_specs=(P("gx", None, "band", None), P("band", None), P()),
        out_specs=P(None, "band", "gx"),
        check_vma=False,
    )
```

profile of v0, /device:TPU:0, one launch (start us, length us, event | category | flops | bytes accessed | tf_op | source)
XLA Modules:
  0.0 213.2 jit_solution(9840836476358481530)
XLA Ops:
  0.0 1.3 collective-permute-start
  2.4 1.3 dynamic-slice_subtract_fusion
  4.8 2.6 %fusion.28 = bf16[8,2,32,2056]{3,2,1,0:T(8,128)(2,1)S(1)} fusion(bf16[4,2,32,2048]{3,2,1,0:T(8,128)(2,1)S(1)} %collective-permute-done, bf16[4,2,32,2048]{3,2,1,0:T(8,128)(2,1)} %param.5), kind=kLoop, calls=%fused_computation.57 | loop fusion | flops 9474048 | bytes 4202496 | tf_op jit(solution)/shard_map/concatenate | solution.py:60
  7.3 108.7 %while.12 = (s32[]{:T(128)}, bf16[12,32,2048]{2,1,0:T(8,128)(2,1)}, f32[32,2056]{1,0:T(8,128)S(1)}, s32[12,2]{0,1:T(2,128)}, bf16[8,2,32,2056]{3,2,1,0:T(8,128)(...) while((s32[]{:T(128)}, bf16[12,32,2048]{2,1,0:T(8,128)(2,1)}, f32[32,2056]{1,0:T(8,128)S(1)}, ...), condition=%wide.region_3.4_spmd, body=%wide.region_2.3_spmd.sunk | while | flops 6569993 | bytes 17456360 | solution.py:69
  13.5 2.2 %slice_add_fusion.9 = f32[4,32,2048]{2,1,0:T(8,128)S(1)} fusion(f32[4,32,2056]{2,1,0:T(8,128)S(1)} %fusion.58), kind=kLoop, calls=%fused_computation.17.clone.1 | loop fusion | flops 2097152 | bytes 10485760 | tf_op jit(solution)/shard_map/while/body/eval_jaxpr/add | solution.py:24
  22.5 2.2 %slice_add_fusion.9 = f32[4,32,2048]{2,1,0:T(8,128)S(1)} fusion(f32[4,32,2056]{2,1,0:T(8,128)S(1)} %fusion.58), kind=kLoop, calls=%fused_computation.17.clone.1 | loop fusion | flops 2097152 | bytes 10485760 | tf_op jit(solution)/shard_map/while/body/eval_jaxpr/add | solution.py:24
  31.6 2.2 %slice_add_fusion.9 = f32[4,32,2048]{2,1,0:T(8,128)S(1)} fusion(f32[4,32,2056]{2,1,0:T(8,128)S(1)} %fusion.58), kind=kLoop, calls=%fused_computation.17.clone.1 | loop fusion | flops 2097152 | bytes 10485760 | tf_op jit(solution)/shard_map/while/body/eval_jaxpr/add | solution.py:24
  40.6 2.2 %slice_add_fusion.9 = f32[4,32,2048]{2,1,0:T(8,128)S(1)} fusion(f32[4,32,2056]{2,1,0:T(8,128)S(1)} %fusion.58), kind=kLoop, calls=%fused_computation.17.clone.1 | loop fusion | flops 2097152 | bytes 10485760 | tf_op jit(solution)/shard_map/while/body/eval_jaxpr/add | solution.py:24
  49.7 2.2 %slice_add_fusion.9 = f32[4,32,2048]{2,1,0:T(8,128)S(1)} fusion(f32[4,32,2056]{2,1,0:T(8,128)S(1)} %fusion.58), kind=kLoop, calls=%fused_computation.17.clone.1 | loop fusion | flops 2097152 | bytes 10485760 | tf_op jit(solution)/shard_map/while/body/eval_jaxpr/add | solution.py:24
  58.7 2.2 %slice_add_fusion.9 = f32[4,32,2048]{2,1,0:T(8,128)S(1)} fusion(f32[4,32,2056]{2,1,0:T(8,128)S(1)} %fusion.58), kind=kLoop, calls=%fused_computation.17.clone.1 | loop fusion | flops 2097152 | bytes 10485760 | tf_op jit(solution)/shard_map/while/body/eval_jaxpr/add | solution.py:24
  67.8 2.2 %slice_add_fusion.9 = f32[4,32,2048]{2,1,0:T(8,128)S(1)} fusion(f32[4,32,2056]{2,1,0:T(8,128)S(1)} %fusion.58), kind=kLoop, calls=%fused_computation.17.clone.1 | loop fusion | flops 2097152 | bytes 10485760 | tf_op jit(solution)/shard_map/while/body/eval_jaxpr/add | solution.py:24
  76.8 2.2 %slice_add_fusion.9 = f32[4,32,2048]{2,1,0:T(8,128)S(1)} fusion(f32[4,32,2056]{2,1,0:T(8,128)S(1)} %fusion.58), kind=kLoop, calls=%fused_computation.17.clone.1 | loop fusion | flops 2097152 | bytes 10485760 | tf_op jit(solution)/shard_map/while/body/eval_jaxpr/add | solution.py:24
  85.9 2.2 %slice_add_fusion.9 = f32[4,32,2048]{2,1,0:T(8,128)S(1)} fusion(f32[4,32,2056]{2,1,0:T(8,128)S(1)} %fusion.58), kind=kLoop, calls=%fused_computation.17.clone.1 | loop fusion | flops 2097152 | bytes 10485760 | tf_op jit(solution)/shard_map/while/body/eval_jaxpr/add | solution.py:24
  95.0 2.2 %slice_add_fusion.9 = f32[4,32,2048]{2,1,0:T(8,128)S(1)} fusion(f32[4,32,2056]{2,1,0:T(8,128)S(1)} %fusion.58), kind=kLoop, calls=%fused_computation.17.clone.1 | loop fusion | flops 2097152 | bytes 10485760 | tf_op jit(solution)/shard_map/while/body/eval_jaxpr/add | solution.py:24
  104.0 2.2 %slice_add_fusion.9 = f32[4,32,2048]{2,1,0:T(8,128)S(1)} fusion(f32[4,32,2056]{2,1,0:T(8,128)S(1)} %fusion.58), kind=kLoop, calls=%fused_computation.17.clone.1 | loop fusion | flops 2097152 | bytes 10485760 | tf_op jit(solution)/shard_map/while/body/eval_jaxpr/add | solution.py:24
  113.1 2.2 %slice_add_fusion.9 = f32[4,32,2048]{2,1,0:T(8,128)S(1)} fusion(f32[4,32,2056]{2,1,0:T(8,128)S(1)} %fusion.58), kind=kLoop, calls=%fused_computation.17.clone.1 | loop fusion | flops 2097152 | bytes 10485760 | tf_op jit(solution)/shard_map/while/body/eval_jaxpr/add | solution.py:24
  116.0 3.0 %copy_bitcast_fusion = bf16[12,32,16,128]{3,1,0,2:T(8,128)(2,1)} fusion(bf16[12,32,2048]{2,1,0:T(8,128)(2,1)} %get-tuple-element.70), kind=kLoop, calls=%fused_computation.62 | loop fusion | bytes 3145728 | tf_op jit(solution)/shard_map/reshape | solution.py:70
  119.0 18.4 %all-to-all-start = ((bf16[12,32,16,128]{3,1,0,2:T(8,128)(2,1)}), bf16[12,32,16,128]{3,1,0,2:T(8,128)(2,1)S(1)}, u32[]{:S(2)}, u32[]{:S(2)}) async-start(bf16[12,32,16,128]{3,1,0,2:T(8,128)(2,1)} %copy_bitcast_fusion), calls=%async_computation | async-start | bytes 3145728 | tf_op jit(solution)/shard_map/all_to_all | solution.py:71
  137.7 5.8 %cholesky.17 = f32[64,64]{1,0:T(8,128)S(1)} custom-call(f32[64,64]{1,0:T(8,128)S(1)} %fusion.41), custom_call_target="Cholesky" | custom-call | tf_op jit(solution)/shard_map/jit(cholesky)/cholesky | solution.py:43
  144.8 4.9 %custom-call.10 = f32[1,64,64]{1,2,0:T(8,128)S(1)} custom-call(f32[1,64,64]{2,1,0:T(8,128)S(1)} %fusion.34), custom_call_target="InvertDiagBlocksLowerTriangular" | custom-call | tf_op jit(solution)/shard_map/jit(_cho_solve)/triangular_solve | solution.py:44
  151.0 18.3 %all-to-all-done = bf16[12,32,16,128]{3,1,0,2:T(8,128)(2,1)S(1)} async-done(((bf16[12,32,16,128]{3,1,0,2:T(8,128)(2,1)}), bf16[12,32,16,128]{3,1,0,2:T(8,128)(2,1)S(1)}, u32[]{:S(2)}, u32[]{:S(2)}) %all-to-all-start) | async-done | bytes 1572896 | tf_op jit(solution)/shard_map/all_to_all | solution.py:71
  170.6 2.5 %fusion.38 = f32[32,128,64]{1,2,0:T(8,128)S(1)} fusion(f32[32,128,64]{2,1,0:T(8,128)S(1)} %fusion.29, f32[1,64,64]{1,2,0:T(8,128)S(1)} %custom-call.10), kind=kOutput, calls=%fused_computation.74 | convolution fusion | flops 201326592 | bytes 2113536 | tf_op jit(solution)/shard_map/jit(_cho_solve)/triangular_solve | solution.py:44
  174.3 37.1 %all-reduce.3 = (f32[64]{0:T(128)S(1)}, f32[64]{0:T(128)S(1)}) all-reduce(f32[64]{0:T(128)S(1)} %get-tuple-element.72, f32[64]{0:T(128)S(1)} %get-tuple-element.71), channel_id=1, replica_groups=mesh['band'=2,'gx'=16] {'gx'}, use_global_device_ids=true, to_apply=%region_7.8 | all-reduce | flops 128 | bytes 1024 | tf_op jit(solution)/shard_map/psum | solution.py:89
  211.7 1.6 copy.8
  (91 shorter events, 44.0 us)
Async XLA Ops:
  0.0 4.8 %collective-permute-start = (bf16[4,2,32,2048]{3,2,1,0:T(8,128)(2,1)}, bf16[4,2,32,2048]{3,2,1,0:T(8,128)(2,1)S(1)}, u32[]{:S(2)}, u32[]{:S(2)}) collective-permute-start(bf16[4,2,32,2048]{3,2,1,0:T(8,128)(2,1)} %param.5), channel_id=1, source_target_pairs={{1,0},{2,1},{3,2},{4,3},{5,4},{6,5},{7,6},{8,7},{9,8},{10,9},{11,1... | collective-permute-start | bytes 3145736 | tf_op jit(solution)/shard_map/ppermute | solution.py:12
  119.0 18.4 %copy-start = (s32[192,2]{0,1:T(2,128)S(1)}, s32[192,2]{0,1:T(2,128)}, u32[]{:S(2)}) copy-start(s32[192,2]{0,1:T(2,128)} %param.7) | copy-start | bytes 4612
  119.0 50.4 %all-to-all-start = ((bf16[12,32,16,128]{3,1,0,2:T(8,128)(2,1)}), bf16[12,32,16,128]{3,1,0,2:T(8,128)(2,1)S(1)}, u32[]{:S(2)}, u32[]{:S(2)}) async-start(bf16[12,32,16,128]{3,1,0,2:T(8,128)(2,1)} %copy_bitcast_fusion), calls=%async_computation | async-start | bytes 3145728 | tf_op jit(solution)/shard_map/all_to_all | solution.py:71
where the time goes:
time: 214 us; the launch traced here: 213 us
  other arithmetic  65.1 us (30%)
  loops' own time  45 us (21%)
  blocking collectives  37.1 us (17%)
  local copies, waits for them, and re-layouts  21.2 us (10%)
  starting transfers between devices  19.7 us (9%)
  waiting for transfers between devices  19.4 us (9%)
  matrix products  5.02 us (2%)
    another operation x1, loops' own time, body(): observed = lax.map(one_pair, own_pairs)  45 us
    psum x1, blocking collectives, body(): totals = lax.psum((partial_mean, partial_slope), 'gx')  37.1 us
    add x12, other arithmetic, box_sum(): summed = summed + running[..., offset:offset + col_count]  26.7 us
    all_to_all x1, starting transfers between devices, body(): lax.all_to_all(blocks, 'gx', split_axis=2, concat_axis=0, tiled=True)  18.4 us
    all_to_all x1, waiting for transfers between devices, body(): lax.all_to_all(blocks, 'gx', split_axis=2, concat_axis=0, tiled=True)  18.3 us
    add x12, other arithmetic, box_sum(): running = running + padded[..., offset:offset + row_count, :]  9.79 us
    dynamic_slice x12, local copies, waits for them, and re-layouts, body(): observed = lax.map(one_pair, own_pairs)  9 us
    dynamic_update_slice x12, other arithmetic, body(): observed = lax.map(one_pair, own_pairs)  8.45 us
  transfers between devices with their start and end apart: 2, of which 2 were waited for; matrix products, arithmetic and copies ran while one was open for 7% of the time, Pallas kernels for 0%

commit v1 on v0

v1 whole, which is shorter than its diff:
```python
import functools
import math

import jax
import jax.numpy as jnp
from jax import lax
from jax.experimental import pallas as pl
from jax.experimental.pallas import tpu as pltpu
from jax.sharding import PartitionSpec as P

LOOK = 9
RIM = LOOK // 2
LAGS = 4
MESH = pl.DeviceIdType.MESH
F32 = jnp.float32
BF16 = jnp.bfloat16
HIGHEST = lax.Precision.HIGHEST
MIB = 1024 * 1024


def greet_all(n, band, me):
    barrier = pltpu.get_barrier_semaphore()

    def greet(k, carry):
        peer = lax.rem(me + k, n)
        pl.semaphore_signal(barrier, inc=1, device_id=(band, peer), device_id_type=MESH)
        return carry

    lax.fori_loop(1, n, greet, 0)
    pl.semaphore_wait(barrier, n - 1)


def network_weights(pairs, dates, degree_bound):
    pair_total = pairs.shape[0]
    first = pairs[:, 0:1]
    second = pairs[:, 1:2]
    ids = lax.broadcasted_iota(jnp.int32, (pair_total, dates), 1)
    incidence_t = (ids == first).astype(F32) - (ids == second).astype(F32)
    incidence = incidence_t.T
    product = jnp.dot(incidence.astype(BF16), incidence_t.astype(BF16), preferred_element_type=F32)
    row = lax.broadcasted_iota(jnp.int32, (dates, dates), 0)
    col = lax.broadcasted_iota(jnp.int32, (dates, dates), 1)
    eye = (row == col).astype(F32)
    normal = product + eye
    top = 1.0 + 2.0 * degree_bound
    scale = 2.0 / (1.0 + top)
    power = eye - normal * scale
    inverse = (eye + power) * scale
    terms = 2
    need = 18.5 * (top + 1.0) / 2.0
    while terms < need:
        power = jnp.dot(power, power, precision=HIGHEST, preferred_element_type=F32)
        inverse = inverse + jnp.dot(inverse, power, precision=HIGHEST, preferred_element_type=F32)
        terms *= 2
    combos = LAGS * dates
    key = first + dates * (second - first - 1)
    combo = lax.broadcasted_iota(jnp.int32, (pair_total, combos), 1)
    count = jnp.sum((combo == key).astype(F32), axis=0, keepdims=True)
    combo = lax.broadcasted_iota(jnp.int32, (dates, combos), 1)
    lag = jnp.ones_like(combo)
    for step in range(1, LAGS):
        lag = lag + (combo >= step * dates).astype(jnp.int32)
    start = combo - dates * (lag - 1)
    date = lax.broadcasted_iota(jnp.int32, (dates, combos), 0)
    spread = ((date == start).astype(F32) - (date == start + lag).astype(F32)) * count
    return jnp.dot(inverse, spread, precision=HIGHEST, preferred_element_type=F32)


def exchange_kernel(
    n, slc, rims, pairs, images, rims_out, weights, send_sem, recv_sem, rim_send, rim_recv, own_sem
):
    band = lax.axis_index("band")
    me = lax.axis_index("gx")
    date_dev = slc.shape[0]
    strip = images.shape[3]
    greet_all(n, band, me)

    def tile_copy(k, source):
        peer = lax.rem(me + k, n)
        return pltpu.make_async_remote_copy(
            src_ref=slc.at[:, :, :, pl.ds(pl.multiple_of(peer * strip, strip), strip)],
            dst_ref=images.at[pl.ds(source * date_dev, date_dev)],
            send_sem=send_sem.at[k],
            recv_sem=recv_sem.at[k],
            device_id=(band, peer),
            device_id_type=MESH,
        )

    def rim_copy(k, source):
        peer = lax.rem(me + k, n)
        return pltpu.make_async_remote_copy(
            src_ref=rims.at[peer],
            dst_ref=rims_out.at[source],
            send_sem=rim_send.at[k],
            recv_sem=rim_recv.at[k],
            device_id=(band, peer),
            device_id_type=MESH,
        )

    def start(k, carry):
        tile_copy(k, me).start()
        rim_copy(k, me).start()
        return carry

    lax.fori_loop(1, n, start, 0)
    own_tile = pltpu.make_async_copy(
        slc.at[:, :, :, pl.ds(pl.multiple_of(me * strip, strip), strip)],
        images.at[pl.ds(me * date_dev, date_dev)],
        own_sem.at[0],
    )
    own_rim = pltpu.make_async_copy(rims.at[me], rims_out.at[me], own_sem.at[1])
    own_tile.start()
    own_rim.start()
    dates = date_dev * n
    weights[...] = network_weights(pairs[...], dates, 2.0 * (pairs.shape[0] // n))

    def finish(k, carry):
        source = lax.rem(me + n - k, n)
        tile = tile_copy(k, source)
        tile.wait_send()
        tile.wait_recv()
        rim = rim_copy(k, source)
        rim.wait_send()
        rim.wait_recv()
        return carry

    lax.fori_loop(1, n, finish, 0)
    own_tile.wait()
    own_rim.wait()


def split(values):
    high = values.astype(BF16)
    low = (values - high.astype(F32)).astype(BF16)
    return high, low


def cross(planes, first, second, rows):
    first = pl.ds(first, rows)
    second = pl.ds(second, rows)
    return planes[3, first, :] * planes[0, second, :] - planes[2, first, :] * planes[1, second, :]


def power(planes, first, rows):
    first = pl.ds(first, rows)
    return planes[2, first, :] * planes[0, first, :] + planes[3, first, :] * planes[1, first, :]


def strip_kernel(
    images, rims, weight, rim_weight, weights, columns, series, sums, planes, rim_planes,
    high, low, rim_high, rim_low, powers, solved
):
    dates, _, rows, strip = images.shape
    pitch = dates + 8
    halves = rows // 16
    devices = rims.shape[0]
    date_dev = dates // devices
    combos = LAGS * dates
    block = 16

    zero = jnp.zeros((8, strip), F32)
    for part in range(4):
        for r in range(rows):
            planes[part, r * pitch + dates : (r + 1) * pitch, :] = zero
        for half in range(halves):
            rim_planes[part, half * pitch + dates : (half + 1) * pitch, :] = zero
    powers[dates:pitch, :] = zero

    def place(t, carry):
        for part in range(2):
            plane = images[t, part].astype(F32)
            heavy = plane * weight[...]
            for q in range(rows // 8):
                target = pl.ds(q * 8 * pitch + t, 8, stride=pitch)
                planes[part, target, :] = plane[q * 8 : q * 8 + 8]
                planes[part + 2, target, :] = heavy[q * 8 : q * 8 + 8]
        return carry

    lax.fori_loop(0, dates, place, 0, unroll=4)

    for d in range(devices):
        tile = rims[d].astype(F32)
        for part in range(2):
            for half in range(halves):
                at = (part * halves + half) * date_dev
                piece = tile[at : at + date_dev]
                target = half * pitch + d * date_dev
                rim_planes[part, target : target + date_dev, :] = piece
                rim_planes[part + 2, target : target + date_dev, :] = (
                    piece * rim_weight[half : half + 1, :]
                )

    def row_sums(b, carry):
        t0 = pl.multiple_of(b * block, block)
        for lag in range(LAGS + 1):
            ones, twos, fours, eights = {}, {}, {}, {}

            def emit(r):
                total = eights.get(r - RIM)
                if r + RIM < rows:
                    total = total + ones[r + RIM]
                h, l = split(total)
                where = pl.ds(pl.multiple_of(lag * dates + t0, block), block)
                high[r, where, :] = h
                low[r, where, :] = l

            for r in range(rows):
                if lag == 0:
                    ones[r] = power(planes, r * pitch + t0, block)
                else:
                    ones[r] = cross(planes, r * pitch + t0, r * pitch + t0 + lag, block)
                twos[r - 1] = ones[r - 1] + ones[r] if r >= 1 else ones[r]
                fours[r - 3] = twos[r - 3] + twos[r - 1] if r >= 2 else twos[r - 1]
                eights[r - 7] = fours[r - 7] + fours[r - 3] if r >= 4 else fours[r - 3]
                if r >= RIM:
                    emit(r - RIM)
            twos[rows - 1] = ones[rows - 1]
            for s in range(rows - 3, rows):
                fours[s] = twos[s] + twos[s + 2] if s + 2 < rows else twos[s]
            for s in range(rows - 7, rows - 4):
                eights[s] = fours[s] + fours[s + 4]
            for r in range(rows - RIM, rows):
                emit(r)
        return carry

    lax.fori_loop(0, dates // block, row_sums, 0)

    pieces = []
    for lag in range(LAGS + 1):
        line = []
        for half in range(halves):
            if lag == 0:
                line.append(power(rim_planes, half * pitch, dates))
            else:
                line.append(cross(rim_planes, half * pitch, half * pitch + lag, dates))
        pieces.append(jnp.concatenate(line, axis=1))
    rim_all = jnp.concatenate(pieces, axis=0)
    lanes = rows * 8
    a = lax.broadcasted_iota(jnp.int32, (lanes, lanes), 0)
    b = lax.broadcasted_iota(jnp.int32, (lanes, lanes), 1)
    near = (jnp.abs((a >> 3) - (b >> 3)) <= RIM) & ((a & 7) == (b & 7))
    near = jnp.where(near, 1.0, 0.0).astype(BF16)
    h, l = split(rim_all)
    rim_sum = jnp.dot(h, near, preferred_element_type=F32) + jnp.dot(
        l, near, preferred_element_type=F32
    )
    h, l = split(rim_sum)
    for half in range(halves):
        rim_high[half] = h[:, half * 128 : half * 128 + 128]
        rim_low[half] = l[:, half * 128 : half * 128 + 128]

    k = lax.broadcasted_iota(jnp.int32, (strip, strip), 0)
    c = lax.broadcasted_iota(jnp.int32, (strip, strip), 1)
    main = jnp.where(jnp.abs(k - c) <= RIM, 1.0, 0.0).astype(BF16)
    k = lax.broadcasted_iota(jnp.int32, (128, strip), 0)
    c = lax.broadcasted_iota(jnp.int32, (128, strip), 1)
    offset = k & 7
    place_col = jnp.where(offset < RIM, offset - RIM, strip + offset - RIM)
    rim_near = jnp.where(jnp.abs(place_col - c) <= RIM, 1.0, 0.0)
    w_high, w_low = split(weights[...])
    mix = jnp.concatenate([w_high, w_low], axis=0)

    def one_row(r, total):
        half = lax.div(r, 16)
        within = lax.rem(r, 16)
        side = jnp.where((k >> 3) == within, rim_near, 0.0).astype(BF16)
        band_matrix = jnp.concatenate([main, side], axis=0)
        looked = jnp.dot(
            jnp.concatenate([high[r], rim_high[half]], axis=1),
            band_matrix,
            preferred_element_type=F32,
        ) + jnp.dot(
            jnp.concatenate([low[r], rim_low[half]], axis=1),
            band_matrix,
            preferred_element_type=F32,
        )
        first = looked[0:dates]
        powers[0:dates, :] = first
        observed = []
        for lag in range(1, LAGS + 1):
            second = powers[lag : lag + dates, :]
            sine = looked[lag * dates : (lag + 1) * dates] * lax.rsqrt(first * second + 1e-6)
            observed.append(sine.astype(BF16))
        both = jnp.dot(mix, jnp.concatenate(observed, axis=0), preferred_element_type=F32)
        value = both[0:dates] + both[dates:]
        solved[pl.ds(pl.multiple_of(r * dates, dates), dates), :] = value
        return total + value

    total = lax.fori_loop(0, rows, one_row, jnp.zeros((dates, strip), F32))
    mean = jnp.sum(total, axis=1, keepdims=True)
    slope = jnp.sum(total * columns[...], axis=1, keepdims=True)
    lane = lax.broadcasted_iota(jnp.int32, (dates, 128), 1)
    sums[...] = jnp.where(lane == 0, mean, slope).T[0:8]

    def unplace(t, carry):
        for q in range(rows // 8):
            series[t, q * 8 : q * 8 + 8, :] = solved[pl.ds(q * 8 * dates + t, 8, stride=dates), :]
        return carry

    lax.fori_loop(0, dates, unplace, 0, unroll=8)


def total_kernel(n, mine, total, slots, send_sem, recv_sem):
    band = lax.axis_index("band")
    me = lax.axis_index("gx")
    greet_all(n, band, me)

    def copy(k, source):
        return pltpu.make_async_remote_copy(
            src_ref=mine,
            dst_ref=slots.at[source],
            send_sem=send_sem.at[k],
            recv_sem=recv_sem.at[k],
            device_id=(band, lax.rem(me + k, n)),
            device_id_type=MESH,
        )

    def start(k, carry):
        copy(k, me).start()
        return carry

    def finish(k, carry):
        one = copy(k, lax.rem(me + n - k, n))
        one.wait_send()
        one.wait_recv()
        return carry

    lax.fori_loop(1, n, start, 0)
    slots[me] = mine[...]
    lax.fori_loop(1, n, finish, 0)
    total[...] = lax.fori_loop(1, n, lambda k, acc: acc + slots[k], slots[0])


def rim_lanes(values, strip):
    lead = values.shape[:-2]
    rows, cols = values.shape[-2:]
    strips = cols // strip
    view = values.reshape(lead + (rows, strips, strip))
    left = view[..., strip - RIM :]
    right = view[..., :RIM]
    gap = jnp.zeros(lead + (rows, 1, RIM), values.dtype)
    left = jnp.concatenate([gap, left[..., :-1, :]], axis=-2)
    right = jnp.concatenate([right[..., 1:, :], gap], axis=-2)
    both = jnp.concatenate([left, right], axis=-1)
    both = jnp.moveaxis(both, -2, 0)
    return both.reshape((strips,) + lead + (rows // 16, 128))


def body(slc_tiles, look_weight, pair_list):
    n = lax.axis_size("gx")
    me = lax.axis_index("gx")
    date_dev, _, rows, cols = slc_tiles.shape
    strip = cols // n
    dates = date_dev * n
    pitch = dates + 8
    halves = rows // 16
    combos = LAGS * dates
    planned = (LAGS + 1) * dates

    rims = rim_lanes(slc_tiles, strip)
    rims = jnp.transpose(rims, (0, 2, 3, 1, 4)).reshape(n, 2 * halves * date_dev, 128)
    weight = lax.dynamic_slice_in_dim(look_weight, me * strip, strip, 1)
    rim_weight = lax.dynamic_index_in_dim(rim_lanes(look_weight, strip), me, 0, keepdims=False)

    vmem = pl.BlockSpec(memory_space=pltpu.VMEM)
    anywhere = pl.BlockSpec(memory_space=pl.ANY)
    dma = pltpu.SemaphoreType.DMA
    images, rims, weights = pl.pallas_call(
        functools.partial(exchange_kernel, n),
        out_shape=(
            jax.ShapeDtypeStruct((dates, 2, rows, strip), BF16),
            jax.ShapeDtypeStruct(rims.shape, BF16),
            jax.ShapeDtypeStruct((dates, combos), F32),
        ),
        in_specs=[anywhere, anywhere, vmem],
        out_specs=(anywhere, anywhere, vmem),
        scratch_shapes=[dma((n,)), dma((n,)), dma((n,)), dma((n,)), dma((2,))],
        compiler_params=pltpu.CompilerParams(
            collective_id=0, has_side_effects=True, vmem_limit_bytes=48 * MIB
        ),
    )(slc_tiles, rims, pair_list)

    column_ids = me * strip + lax.iota(jnp.int32, strip)
    columns = (2.0 * column_ids.astype(F32) + 1.0) / cols - 1.0
    series, sums = pl.pallas_call(
        strip_kernel,
        out_shape=(
            jax.ShapeDtypeStruct((dates, rows, strip), F32),
            jax.ShapeDtypeStruct((8, dates), F32),
        ),
        in_specs=[vmem] * 6,
        out_specs=(vmem, vmem),
        scratch_shapes=[
            pltpu.VMEM((4, rows * pitch, strip), F32),
            pltpu.VMEM((4, halves * pitch, 128), F32),
            pltpu.VMEM((rows, planned, strip), BF16),
            pltpu.VMEM((rows, planned, strip), BF16),
            pltpu.VMEM((halves, planned, 128), BF16),
            pltpu.VMEM((halves, planned, 128), BF16),
            pltpu.VMEM((pitch, strip), F32),
            pltpu.VMEM((rows * dates, strip), F32),
        ],
        compiler_params=pltpu.CompilerParams(vmem_limit_bytes=60 * MIB),
    )(images, rims, weight, rim_weight, weights, columns[None, :])

    totals = pl.pallas_call(
        functools.partial(total_kernel, n),
        out_shape=jax.ShapeDtypeStruct((8, dates), F32),
        in_specs=[vmem],
        out_specs=vmem,
        scratch_shapes=[pltpu.VMEM((n, 8, dates), F32), dma((n,)), dma((n,))],
        compiler_params=pltpu.CompilerParams(collective_id=1, has_side_effects=True),
    )(sums)

    all_cols = (2.0 * lax.iota(jnp.int32, cols).astype(F32) + 1.0) / cols - 1.0
    square_sum = jnp.sum(all_cols * all_cols)
    date_mean = totals[0] / (rows * cols)
    date_slope = totals[1] / (rows * square_sum)
    return series - date_mean[:, None, None] - date_slope[:, None, None] * columns


def solution(mesh):
    return jax.shard_map(
        body,
        mesh=mesh,
        in_specs=(P("gx", None, "band", None), P("band", None), P()),
        out_specs=P(None, "band", "gx"),
        check_vma=False,
    )
```

time: 214 us -> 76 us (0.36)
  other arithmetic: 65.1 us -> 4.95 us
  Pallas kernels: 0 us -> 59.4 us
  loops' own time: 45 us -> 0 us
  blocking collectives: 37.1 us -> 0 us
  starting transfers between devices: 19.7 us -> 0 us
  waiting for transfers between devices: 19.4 us -> 0 us
  local copies, waits for them, and re-layouts: 21.2 us -> 10.6 us
  matrix products: 5.02 us -> 0 us
    pallas_call x0 -> x3, Pallas kernels: none -> 59.4 us  [the longest x1 25.1 us: body(): pl.pallas_call(functools.partial(exchange_kernel, n), out_shape=(jax.Shap...]
    another operation x1 -> x0, loops' own time: 45 us -> none  [body(): observed = lax.map(one_pair, own_pairs)]
    psum x1 -> x0, blocking collectives: 37.1 us -> none  [body(): totals = lax.psum((partial_mean, partial_slope), 'gx')]
    add x24 -> x0, other arithmetic: 36.4 us -> none  [the longest x12 26.7 us: box_sum(): summed = summed + running[..., offset:offset + col_count]]
    all_to_all x1 -> x0, starting transfers between devices: 18.4 us -> none  [body(): lax.all_to_all(blocks, 'gx', split_axis=2, concat_axis=0, tiled=True)]
    all_to_all x1 -> x0, waiting for transfers between devices: 18.3 us -> none  [body(): lax.all_to_all(blocks, 'gx', split_axis=2, concat_axis=0, tiled=True)]
    another operation x17 -> x0, other arithmetic: 13 us -> none  [the longest x3 6.52 us: solve_normal(): factor = jnp.linalg.cholesky(normal_matrix)]
    dynamic_update_slice x12 -> x0, other arithmetic: 8.45 us -> none  [body(): observed = lax.map(one_pair, own_pairs)]
  transfers between devices with their start and end apart: 2 -> 0, of which waited for: 2 -> 0; matrix products, arithmetic and copies ran while one was open for 7% -> 0% of each run, Pallas kernels for 0% -> 0%
where the time goes in v1:
time: 76 us; the launch traced here: 75.7 us
  Pallas kernels  59.4 us (78%)
  local copies, waits for them, and re-layouts  10.6 us (14%)
  other arithmetic  4.95 us (7%)
  between operations  0.76 us (1%)
    pallas_call x1, Pallas kernels, body(): pl.pallas_call(functools.partial(exchange_kernel, n), out_shape=(jax.Shap...  25.1 us
    pallas_call x1, Pallas kernels, body(): pl.pallas_call(strip_kernel, out_shape=(jax.ShapeDtypeStruct((dates, rows...  20.6 us
    pallas_call x1, Pallas kernels, body(): pl.pallas_call(functools.partial(total_kernel, n), out_shape=jax.ShapeDty...  13.7 us
    unnamed x19, local copies, waits for them, and re-layouts  8.13 us
    sub x1, other arithmetic, body(): series - date_mean[:, None, None] - date_slope[:, None, None] * columns  2.35 us

profile of v1, /device:TPU:0, one launch (start us, length us, event | category | flops | bytes accessed | tf_op | source)
XLA Modules:
  0.0 75.7 jit_solution(562012380673381149)
XLA Ops:
  0.0 1.5 %copy.22 = bf16[32,8,16,128]{3,2,1,0:T(8,128)(2,1)S(1)} copy(bf16[32,8,16,128]{3,1,2,0:T(8,128)(2,1)} %bitcast.20) | data formatting | bytes 2097152
  1.5 0.8 %fusion.3 = (bf16[4,2,32,15,4]{4,3,2,1,0:T(8,128)(2,1)S(1)}, bf16[4,2,32,15,4]{4,3,2,1,0:T(8,128)(2,1)S(1)}) fusion(bf16[4,2,32,16,128]{4,3,2,1,0:T(8,128)(2,1)S(1)} %bitcast.22), kind=kLoop, calls=%fused_computation.17 | loop fusion | bytes 122880 | tf_op jit(solution)/shard_map/slice | solution.py:342
  2.3 1.6 %copy.19 = bf16[4,2,32,15,4]{3,4,2,1,0:T(4,128)(2,1)S(1)} copy(bf16[4,2,32,15,4]{4,3,2,1,0:T(8,128)(2,1)S(1)} %get-tuple-element.16) | data formatting | bytes 61440
  3.9 1.6 %copy.18 = bf16[4,2,32,15,4]{3,4,2,1,0:T(4,128)(2,1)S(1)} copy(bf16[4,2,32,15,4]{4,3,2,1,0:T(8,128)(2,1)S(1)} %get-tuple-element.15) | data formatting | bytes 61440
  5.5 0.5 fusion.2
  6.0 0.2 copy.14
  6.2 0.5 copy-done.5
  6.7 0.1 copy.15.pairs
  6.8 25.1 %shard_map.37 = (bf16[64,2,32,128]{3,2,1,0:T(8,128)(2,1)S(1)}, bf16[16,16,128]{2,1,0:T(8,128)(2,1)S(1)}, f32[64,256]{1,0:T(8,128)S(1)}) custom-call(bf16[4,2,32,2048]{3,2,1,0:T(8,128)(2,1)S(1)} %copy-done, bf16[16,16,128]{2,1,0:T(8,128)(2,1)S(1)} %bitcast.21, s32[192,2]{1,0:T(8,128)S(1)} %copy.15.pairs), custom_call_target="tpu_custom_call" | custom-call | tf_op jit(solution)/shard_map/pallas_call | solution.py:368
  32.0 1.0 %copy-done.1 = bf16[64,2,32,128]{3,2,1,0:T(8,128)(2,1)} copy-done((bf16[64,2,32,128]{3,2,1,0:T(8,128)(2,1)}, bf16[64,2,32,128]{3,2,1,0:T(8,128)(2,1)S(1)}, u32[]{:S(2)}) %copy-start.1) | copy-done | bytes 1048600
  33.0 0.6 copy-done.2
  33.6 0.6 copy-done.3
  34.2 0.6 constant_dynamic-slice_fusion.weight
  34.9 0.1 fusion.4
  35.0 0.3 copy.21
  35.3 0.3 copy.20
  35.6 0.1 select_maximum_fusion
  35.7 0.7 dynamic-slice_reduce_fusion.rim_weight
  36.5 0.5 multiply_add_fusion.1.columns
  37.0 20.6 %shard_map.38 = (f32[64,32,128]{2,1,0:T(8,128)}, f32[8,64]{1,0:T(8,128)}) custom-call(bf16[64,2,32,128]{3,2,1,0:T(8,128)(2,1)} %copy-done.1, bf16[16,16,128]{2,1,0:T(8,128)(2,1)} %copy-done.2, f32[32,128]{1,0:T(8,128)} %constant_dynamic-slice_fusion.weight, f32[2,128]{1,0:T(2,128)} %dynamic-slice_reduce_fusion.rim_weight, f32[64,256]{1,0:T(8,128)} %copy-done.3, ...), custom_call_target="tpu_custom_call" | custom-call | tf_op jit(solution)/shard_map/pallas_call | solution.py:385
  57.6 13.7 %shard_map.39 = f32[8,64]{1,0:T(8,128)} custom-call(f32[8,64]{1,0:T(8,128)} %get-tuple-element.14.mine), custom_call_target="tpu_custom_call" | custom-call | tf_op jit(solution)/shard_map/pallas_call | solution.py:406
  71.3 0.6 multiply_reduce_fusion
  72.6 0.8 multiply_bitcast_fusion
  73.4 2.4 %subtract_subtract_fusion = f32[64,32,128]{2,1,0:T(8,128)} fusion(f32[64,32,128]{2,1,0:T(8,128)} %get-tuple-element.13, f32[64,128]{1,0:T(8,128)S(1)} %broadcast_multiply_fusion, f32[64]{0:T(128)S(1)} %get-tuple-element.19), kind=kLoop, calls=%fused_computation.2 | loop fusion | flops 524288 | bytes 2130176 | tf_op jit(solution)/shard_map/sub | solution.py:419
  (11 shorter events, 0.2 us)
Async XLA Ops:
  5.5 1.3 %copy-start = (bf16[4,2,32,2048]{3,2,1,0:T(8,128)(2,1)S(1)}, bf16[4,2,32,2048]{3,2,1,0:T(8,128)(2,1)}, u32[]{:S(2)}) copy-start(bf16[4,2,32,2048]{3,2,1,0:T(8,128)(2,1)} %slc.1) | copy-start | bytes 3145732
  6.0 0.7 copy-start.5
  6.8 27.4 %copy-start.4 = (f32[32,2048]{1,0:T(8,128)S(1)}, f32[32,2048]{1,0:T(8,128)}, u32[]{:S(2)}) copy-start(f32[32,2048]{1,0:T(8,128)} %param.4) | copy-start | bytes 786436
  32.0 1.0 %copy-start.1 = (bf16[64,2,32,128]{3,2,1,0:T(8,128)(2,1)}, bf16[64,2,32,128]{3,2,1,0:T(8,128)(2,1)S(1)}, u32[]{:S(2)}) copy-start(bf16[64,2,32,128]{3,2,1,0:T(8,128)(2,1)S(1)} %get-tuple-element.10.images) | copy-start | bytes 3145732
  33.0 0.6 copy-start.2
  33.6 0.6 copy-start.3

commit v2 on v0

v2 whole, which is shorter than its diff:
```python
import functools
import math

import jax
import jax.numpy as jnp
from jax import lax
from jax.experimental import pallas as pl
from jax.experimental.pallas import tpu as pltpu
from jax.sharding import PartitionSpec as P

LOOK = 9
RIM = LOOK // 2
LAGS = 4
MESH = pl.DeviceIdType.MESH
F32 = jnp.float32
BF16 = jnp.bfloat16
HIGHEST = lax.Precision.HIGHEST
MIB = 1024 * 1024


def greet_all(n, band, me):
    barrier = pltpu.get_barrier_semaphore()

    def greet(k, carry):
        peer = lax.rem(me + k, n)
        pl.semaphore_signal(barrier, inc=1, device_id=(band, peer), device_id_type=MESH)
        return carry

    lax.fori_loop(1, n, greet, 0)
    pl.semaphore_wait(barrier, n - 1)


def network_weights(pairs, dates, degree_bound):
    pair_total = pairs.shape[0]
    first = pairs[:, 0:1]
    second = pairs[:, 1:2]
    ids = lax.broadcasted_iota(jnp.int32, (pair_total, dates), 1)
    incidence_t = (ids == first).astype(F32) - (ids == second).astype(F32)
    incidence = incidence_t.T
    product = jnp.dot(incidence.astype(BF16), incidence_t.astype(BF16), preferred_element_type=F32)
    row = lax.broadcasted_iota(jnp.int32, (dates, dates), 0)
    col = lax.broadcasted_iota(jnp.int32, (dates, dates), 1)
    eye = (row == col).astype(F32)
    normal = product + eye
    top = 1.0 + 2.0 * degree_bound
    scale = 2.0 / (1.0 + top)
    power = eye - normal * scale
    inverse = (eye + power) * scale
    terms = 2
    need = 18.5 * (top + 1.0) / 2.0
    while terms < need:
        power = jnp.dot(power, power, precision=HIGHEST, preferred_element_type=F32)
        inverse = inverse + jnp.dot(inverse, power, precision=HIGHEST, preferred_element_type=F32)
        terms *= 2
    combos = LAGS * dates
    key = first + dates * (second - first - 1)
    combo = lax.broadcasted_iota(jnp.int32, (pair_total, combos), 1)
    count = jnp.sum((combo == key).astype(F32), axis=0, keepdims=True)
    combo = lax.broadcasted_iota(jnp.int32, (dates, combos), 1)
    lag = jnp.ones_like(combo)
    for step in range(1, LAGS):
        lag = lag + (combo >= step * dates).astype(jnp.int32)
    start = combo - dates * (lag - 1)
    date = lax.broadcasted_iota(jnp.int32, (dates, combos), 0)
    spread = ((date == start).astype(F32) - (date == start + lag).astype(F32)) * count
    return jnp.dot(inverse, spread, precision=HIGHEST, preferred_element_type=F32)


def split(values):
    high = values.astype(BF16)
    low = (values - high.astype(F32)).astype(BF16)
    return high, low


def cross(planes, first, second, rows):
    first = pl.ds(first, rows)
    second = pl.ds(second, rows)
    return planes[3, first, :] * planes[0, second, :] - planes[2, first, :] * planes[1, second, :]


def power(planes, first, rows):
    first = pl.ds(first, rows)
    return planes[2, first, :] * planes[0, first, :] + planes[3, first, :] * planes[1, first, :]


def window_sums(term, lo, hi, out_lo, out_hi):
    @functools.cache
    def ones(r):
        return term(r) if lo <= r < hi else None

    @functools.cache
    def run(r, size):
        if size == 1:
            return ones(r)
        a, b = run(r, size // 2), run(r + size // 2, size // 2)
        return b if a is None else a if b is None else a + b

    for r in range(out_lo, out_hi):
        total, last = run(r - RIM, LOOK - 1), ones(r + RIM)
        yield r, total if last is None else total + last


def kernel(
    n, slc, look_weight, pairs, series,
    local, images, rim_parts, rim_send, rim_recv, weight, weights, planes, rim_planes,
    high, low, rim_high, rim_low, powers, solved, mine, slots, trend,
    send_sem, recv_sem, own_sem,
):
    band = lax.axis_index("band")
    me = lax.axis_index("gx")
    date_dev, _, rows, cols = slc.shape
    halves, dates, _, block, strip = images.shape
    pitch = dates + 8
    groups = date_dev * 2 * halves

    def columns_of(j):
        return pl.ds(pl.multiple_of(j * strip, strip), strip)

    fetch = pltpu.make_async_copy(slc, local, own_sem.at[0])
    fetch.start()
    sides = (lax.max(me - 1, 0), me, lax.min(me + 1, n - 1))
    weight_copies = [
        pltpu.make_async_copy(look_weight.at[:, columns_of(j)], weight.at[i], own_sem.at[1 + i])
        for i, j in enumerate(sides)
    ]
    for copy in weight_copies:
        copy.start()
    own_tiles = [
        pltpu.make_async_copy(
            slc.at[:, :, pl.ds(h * block, block), columns_of(me)],
            images.at[h, pl.ds(me * date_dev, date_dev)],
            own_sem.at[4 + h],
        )
        for h in range(halves)
    ]
    for copy in own_tiles:
        copy.start()
    greet_all(n, band, me)

    def tile_copy(h, k, source):
        peer = lax.rem(me + k, n)
        return pltpu.make_async_remote_copy(
            src_ref=slc.at[:, :, pl.ds(h * block, block), columns_of(peer)],
            dst_ref=images.at[h, pl.ds(source * date_dev, date_dev)],
            send_sem=send_sem.at[h, k],
            recv_sem=recv_sem.at[h, k],
            device_id=(band, peer),
            device_id_type=MESH,
        )

    def rim_copy(k, source):
        peer = lax.rem(me + k, n)
        return pltpu.make_async_remote_copy(
            src_ref=rim_send.at[peer],
            dst_ref=rim_recv.at[source],
            send_sem=send_sem.at[halves, k],
            recv_sem=recv_sem.at[halves, k],
            device_id=(band, peer),
            device_id_type=MESH,
        )

    def sum_copy(k, source):
        return pltpu.make_async_remote_copy(
            src_ref=mine,
            dst_ref=slots.at[source],
            send_sem=send_sem.at[halves + 1, k],
            recv_sem=recv_sem.at[halves + 1, k],
            device_id=(band, lax.rem(me + k, n)),
            device_id_type=MESH,
        )

    def start_all(make):
        def start(k, carry):
            make(k, me).start()
            return carry

        lax.fori_loop(1, n, start, 0)

    def finish_all(make):
        def finish(k, carry):
            one = make(k, lax.rem(me + n - k, n))
            one.wait_send()
            one.wait_recv()
            return carry

        lax.fori_loop(1, n, finish, 0)

    start_all(functools.partial(tile_copy, 0))

    a = lax.broadcasted_iota(jnp.int32, (strip, 256), 0)
    b = lax.broadcasted_iota(jnp.int32, (strip, 256), 1)
    h = b & 7
    pick = ((b < 128) & (h < RIM) & (a == strip - RIM + h)) | (
        (b >= 128) & (h >= RIM) & (a == h - RIM)
    )
    pick = jnp.where(pick, 1.0, 0.0)
    pick_half = pick.astype(BF16)
    tall = groups * block
    a = lax.broadcasted_iota(jnp.int32, (tall, 256), 0)
    b = lax.broadcasted_iota(jnp.int32, (tall, 256), 1)
    keep = jnp.where((a & (block - 1)) == ((b & 127) >> 3), 1.0, 0.0)
    a = lax.broadcasted_iota(jnp.int32, (groups, tall), 0)
    b = lax.broadcasted_iota(jnp.int32, (groups, tall), 1) >> 4
    gather = jnp.zeros((groups, tall), jnp.bool_)
    for d in range(date_dev):
        for ph in range(2 * halves):
            gather = gather | ((b == d * 2 * halves + ph) & (a == ph * date_dev + d))
    gather = jnp.where(gather, 1.0, 0.0).astype(BF16)
    empty = jnp.zeros((groups, 256), F32)
    rim_parts[0] = empty
    rim_parts[n + 1] = empty
    fetch.wait()

    def pick_rims(j, carry):
        slab = local[:, :, :, columns_of(j)].reshape(tall, strip)
        spread = jnp.dot(slab, pick_half, preferred_element_type=F32) * keep
        rim_parts[j + 1] = jnp.dot(gather, spread.astype(BF16), preferred_element_type=F32)
        return carry

    lax.fori_loop(0, n, pick_rims, 0)

    def join_rims(j, carry):
        rim_send[j] = (rim_parts[j, :, 0:128] + rim_parts[j + 2, :, 128:256]).astype(BF16)
        return carry

    lax.fori_loop(0, n, join_rims, 0)
    start_all(rim_copy)
    for half in range(1, halves):
        start_all(functools.partial(tile_copy, half))
    rim_recv[me] = rim_send[me]

    weights[...] = network_weights(pairs[...], dates, 2.0 * (pairs.shape[0] // n))
    w_high, w_low = split(weights[...])
    mix = jnp.concatenate([w_high, w_low], axis=0)
    column_ids = me * strip + lax.broadcasted_iota(jnp.int32, (1, strip), 1)
    columns = (2.0 * column_ids.astype(F32) + 1.0) / cols - 1.0

    for copy in weight_copies:
        copy.wait()
    rim_weight = jnp.dot(
        weight[0], pick[:, 0:128], precision=HIGHEST, preferred_element_type=F32
    ) + jnp.dot(weight[2], pick[:, 128:256], precision=HIGHEST, preferred_element_type=F32)

    zero = jnp.zeros((8, strip), F32)
    for part in range(4):
        for r in range(rows):
            planes[part, r * pitch + dates : (r + 1) * pitch, :] = zero
        for half in range(halves):
            rim_planes[part, half * pitch + dates : (half + 1) * pitch, :] = zero
    for slot in range(powers.shape[0]):
        powers[slot, dates:pitch, :] = zero

    def place_half(half):
        def place(t, carry):
            for part in range(2):
                plane = images[half, t, part].astype(F32)
                heavy = plane * weight[1, half * block : half * block + block, :]
                for q in range(block // 8):
                    row = half * block + q * 8
                    target = pl.ds(row * pitch + t, 8, stride=pitch)
                    planes[part, target, :] = plane[q * 8 : q * 8 + 8]
                    planes[part + 2, target, :] = heavy[q * 8 : q * 8 + 8]
            return carry

        lax.fori_loop(0, dates, place, 0, unroll=4)

    k = lax.broadcasted_iota(jnp.int32, (strip, strip), 0)
    c = lax.broadcasted_iota(jnp.int32, (strip, strip), 1)
    main = jnp.where(jnp.abs(k - c) <= RIM, 1.0, 0.0).astype(BF16)
    k = lax.broadcasted_iota(jnp.int32, (128, strip), 0)
    c = lax.broadcasted_iota(jnp.int32, (128, strip), 1)
    offset = k & 7
    rim_col = jnp.where(offset < RIM, offset - RIM, strip + offset - RIM)
    rim_near = jnp.where(jnp.abs(rim_col - c) <= RIM, 1.0, 0.0)
    together = powers.shape[0]

    def stage(lo, hi, out_lo, out_hi, total):
        def row_sums(b, carry):
            t0 = pl.multiple_of(b * block, block)
            for lag in range(LAGS + 1):
                where = pl.ds(pl.multiple_of(lag * dates + t0, block), block)

                def term(r):
                    first = r * pitch + t0
                    if lag == 0:
                        return power(planes, first, block)
                    return cross(planes, first, first + lag, block)

                for r, value in window_sums(term, lo, hi, out_lo, out_hi):
                    h, l = split(value)
                    high[r - out_lo, where, :] = h
                    low[r - out_lo, where, :] = l
            return carry

        lax.fori_loop(0, dates // block, row_sums, 0)

        def some_rows(g, total):
            looks = []
            for i in range(together):
                at = g * together + i
                r = at + out_lo
                half = lax.div(r, block)
                side = jnp.where((k >> 3) == lax.rem(r, block), rim_near, 0.0).astype(BF16)
                matrix = jnp.concatenate([main, side], axis=0)
                looked = jnp.dot(
                    jnp.concatenate([high[at], rim_high[half]], axis=1),
                    matrix,
                    preferred_element_type=F32,
                ) + jnp.dot(
                    jnp.concatenate([low[at], rim_low[half]], axis=1),
                    matrix,
                    preferred_element_type=F32,
                )
                powers[i, 0:dates, :] = looked[0:dates]
                looks.append(looked)
            sines = []
            for i in range(together):
                looked = looks[i]
                observed = []
                for lag in range(1, LAGS + 1):
                    both = looked[0:dates] * powers[i, lag : lag + dates, :]
                    sine = looked[lag * dates : (lag + 1) * dates] * lax.rsqrt(both + 1e-6)
                    observed.append(sine.astype(BF16))
                sines.append(jnp.concatenate(observed, axis=0))
            for i in range(0, together, 2):
                pair = jnp.concatenate(sines[i : i + 2], axis=1)
                both = jnp.dot(mix, pair, preferred_element_type=F32)
                value = both[0:dates] + both[dates:]
                for e in range(2):
                    r = g * together + i + e + out_lo
                    one = value[:, e * strip : (e + 1) * strip]
                    solved[pl.ds(pl.multiple_of(r * dates, dates), dates), :] = one
                    total = total + one
            return total

        return lax.fori_loop(0, (out_hi - out_lo) // together, some_rows, total)

    finish_all(functools.partial(tile_copy, 0))
    own_tiles[0].wait()
    place_half(0)
    finish_all(rim_copy)

    a = lax.broadcasted_iota(jnp.int32, (rows, 128), 0)
    b = lax.broadcasted_iota(jnp.int32, (rows, 128), 1)
    rim_weight = jnp.where((a & (block - 1)) == (b >> 3), rim_weight, 0.0)
    for half in range(halves):
        heavy = jnp.sum(rim_weight[half * block : half * block + block], axis=0, keepdims=True)
        for d in range(n):
            for part in range(2):
                at = (part * halves + half) * date_dev
                piece = rim_recv[d].astype(F32)[at : at + date_dev]
                target = half * pitch + d * date_dev
                rim_planes[part, target : target + date_dev, :] = piece
                rim_planes[part + 2, target : target + date_dev, :] = piece * heavy
    pieces = []
    for lag in range(LAGS + 1):
        line = []
        for half in range(halves):
            if lag == 0:
                line.append(power(rim_planes, half * pitch, dates))
            else:
                line.append(cross(rim_planes, half * pitch, half * pitch + lag, dates))
        pieces.append(jnp.concatenate(line, axis=1))
    lanes = rows * 8
    a = lax.broadcasted_iota(jnp.int32, (lanes, lanes), 0)
    b = lax.broadcasted_iota(jnp.int32, (lanes, lanes), 1)
    near = (jnp.abs((a >> 3) - (b >> 3)) <= RIM) & ((a & 7) == (b & 7))
    near = jnp.where(near, 1.0, 0.0).astype(BF16)
    h, l = split(jnp.concatenate(pieces, axis=0))
    rim_sum = jnp.dot(h, near, preferred_element_type=F32) + jnp.dot(
        l, near, preferred_element_type=F32
    )
    h, l = split(rim_sum)
    for half in range(halves):
        rim_high[half] = h[:, half * 128 : half * 128 + 128]
        rim_low[half] = l[:, half * 128 : half * 128 + 128]

    total = jnp.zeros((dates, strip), F32)
    ready = block - RIM
    total = stage(0, block, 0, ready, total)
    for half in range(1, halves):
        finish_all(functools.partial(tile_copy, half))
        own_tiles[half].wait()
        place_half(half)
    total = stage(ready - RIM, rows, ready, rows, total)

    mean = jnp.sum(total, axis=1, keepdims=True)
    slope = jnp.sum(total * columns, axis=1, keepdims=True)
    lane = lax.broadcasted_iota(jnp.int32, (dates, 128), 1)
    mine[...] = jnp.where(lane == 0, mean, slope).T[0:8]
    start_all(sum_copy)
    slots[me] = mine[...]
    all_cols = lax.broadcasted_iota(jnp.int32, (1, cols), 1)
    all_cols = (2.0 * all_cols.astype(F32) + 1.0) / cols - 1.0
    square_sum = jnp.sum(all_cols * all_cols, axis=1, keepdims=True)
    finish_all(sum_copy)
    sums = lax.fori_loop(1, n, lambda s, acc: acc + slots[s], slots[0]).T
    date_mean = sums[:, 0:1] / (rows * cols)
    date_slope = sums[:, 1:2] / (rows * square_sum)
    trend[...] = date_mean + date_slope * columns

    def unplace(t, carry):
        gone = trend[pl.ds(t, 1), :]
        for q in range(rows // 8):
            piece = solved[pl.ds(q * 8 * dates + t, 8, stride=dates), :]
            series[t, q * 8 : q * 8 + 8, :] = piece - gone
        return carry

    lax.fori_loop(0, dates, unplace, 0, unroll=8)


def body(slc_tiles, look_weight, pair_list):
    n = lax.axis_size("gx")
    date_dev, _, rows, cols = slc_tiles.shape
    block = 16
    strip = cols // n
    dates = date_dev * n
    pitch = dates + 8
    halves = rows // block
    planned = (LAGS + 1) * dates
    most = rows - block + RIM
    lines = 2 * halves * date_dev

    vmem = pl.BlockSpec(memory_space=pltpu.VMEM)
    anywhere = pl.BlockSpec(memory_space=pl.ANY)
    dma = pltpu.SemaphoreType.DMA
    return pl.pallas_call(
        functools.partial(kernel, n),
        out_shape=jax.ShapeDtypeStruct((dates, rows, strip), F32),
        in_specs=[anywhere, anywhere, vmem],
        out_specs=vmem,
        scratch_shapes=[
            pltpu.VMEM(slc_tiles.shape, BF16),
            pltpu.VMEM((halves, dates, 2, block, strip), BF16),
            pltpu.VMEM((n + 2, lines, 256), F32),
            pltpu.VMEM((n, lines, 128), BF16),
            pltpu.VMEM((n, lines, 128), BF16),
            pltpu.VMEM((3, rows, strip), F32),
            pltpu.VMEM((dates, LAGS * dates), F32),
            pltpu.VMEM((4, rows * pitch, strip), F32),
            pltpu.VMEM((4, halves * pitch, 128), F32),
            pltpu.VMEM((most, planned, strip), BF16),
            pltpu.VMEM((most, planned, strip), BF16),
            pltpu.VMEM((halves, planned, 128), BF16),
            pltpu.VMEM((halves, planned, 128), BF16),
            pltpu.VMEM((4, pitch, strip), F32),
            pltpu.VMEM((rows * dates, strip), F32),
            pltpu.VMEM((8, dates), F32),
            pltpu.VMEM((n, 8, dates), F32),
            pltpu.VMEM((dates, strip), F32),
            dma((halves + 2, n)),
            dma((halves + 2, n)),
            dma((4 + halves,)),
        ],
        compiler_params=pltpu.CompilerParams(
            collective_id=0, has_side_effects=True, vmem_limit_bytes=60 * MIB
        ),
    )(slc_tiles, look_weight, pair_list)


def solution(mesh):
    return jax.shard_map(
        body,
        mesh=mesh,
        in_specs=(P("gx", None, "band", None), P("band", None), P()),
        out_specs=P(None, "band", "gx"),
        check_vma=False,
    )
```

time: 214 us -> 49.2 us (0.23)
  other arithmetic: 65.1 us -> 0 us
  Pallas kernels: 0 us -> 45.3 us
  loops' own time: 45 us -> 0 us
  blocking collectives: 37.1 us -> 0 us
  starting transfers between devices: 19.7 us -> 0 us
  waiting for transfers between devices: 19.4 us -> 0 us
  local copies, waits for them, and re-layouts: 21.2 us -> 3.71 us
  matrix products: 5.02 us -> 0 us
    pallas_call x0 -> x1, Pallas kernels: none -> 45.3 us  [body(): pl.pallas_call(functools.partial(kernel, n), out_shape=jax.ShapeDtypeStru...]
    another operation x1 -> x0, loops' own time: 45 us -> none  [body(): observed = lax.map(one_pair, own_pairs)]
    psum x1 -> x0, blocking collectives: 37.1 us -> none  [body(): totals = lax.psum((partial_mean, partial_slope), 'gx')]
    add x24 -> x0, other arithmetic: 36.4 us -> none  [the longest x12 26.7 us: box_sum(): summed = summed + running[..., offset:offset + col_count]]
    all_to_all x1 -> x0, starting transfers between devices: 18.4 us -> none  [body(): lax.all_to_all(blocks, 'gx', split_axis=2, concat_axis=0, tiled=True)]
    all_to_all x1 -> x0, waiting for transfers between devices: 18.3 us -> none  [body(): lax.all_to_all(blocks, 'gx', split_axis=2, concat_axis=0, tiled=True)]
    another operation x17 -> x0, other arithmetic: 13 us -> none  [the longest x3 6.52 us: solve_normal(): factor = jnp.linalg.cholesky(normal_matrix)]
    dynamic_slice x12 -> x0, local copies, waits for them, and re-layouts: 9 us -> none  [body(): observed = lax.map(one_pair, own_pairs)]
  transfers between devices with their start and end apart: 2 -> 0, of which waited for: 2 -> 0; matrix products, arithmetic and copies ran while one was open for 7% -> 0% of each run, Pallas kernels for 0% -> 0%
where the time goes in v2:
time: 49.2 us; the launch traced here: 49 us
  Pallas kernels  45.3 us (92%)
  local copies, waits for them, and re-layouts  3.71 us (8%)
    pallas_call x1, Pallas kernels, body(): pl.pallas_call(functools.partial(kernel, n), out_shape=jax.ShapeDtypeStru...  45.3 us
    unnamed x2, local copies, waits for them, and re-layouts  3.71 us

profile of v2, /device:TPU:0, one launch (start us, length us, event | category | flops | bytes accessed | tf_op | source)
XLA Modules:
  0.0 49.0 jit_solution(10741101162360409724)
XLA Ops:
  0.0 1.4 %copy.4.pairs = s32[192,2]{1,0:T(8,128)} copy(s32[192,2]{0,1:T(2,128)} %param.5) | data formatting | bytes 3072 | tf_op args[2]
  1.4 45.3 %shard_map.37 = f32[64,32,128]{2,1,0:T(8,128)} custom-call(bf16[4,2,32,2048]{3,2,1,0:T(8,128)(2,1)} %slc.1, f32[32,2048]{1,0:T(8,128)} %look_weight.1, s32[192,2]{1,0:T(8,128)} %copy.4.pairs), custom_call_target="tpu_custom_call" | custom-call | tf_op jit(solution)/shard_map/pallas_call | solution.py:427
  46.8 2.3 %copy.6 = f32[64,32,128]{2,1,0:T(8,128)} copy(f32[64,32,128]{2,1,0:T(8,128)} %shard_map.37) | data formatting | bytes 2097152

commit v3 on v2

--- a/solution.py
+++ b/solution.py
@@ -31,12 +31,12 @@
 
 
 def network_weights(pairs, dates, degree_bound):
-    pair_total = pairs.shape[0]
-    first = pairs[:, 0:1]
-    second = pairs[:, 1:2]
-    ids = lax.broadcasted_iota(jnp.int32, (pair_total, dates), 1)
-    incidence_t = (ids == first).astype(F32) - (ids == second).astype(F32)
-    incidence = incidence_t.T
+    pair_total = pairs.shape[1]
+    first = pairs[0:1]
+    second = pairs[1:2]
+    ids = lax.broadcasted_iota(jnp.int32, (dates, pair_total), 0)
+    incidence = (ids == first).astype(F32) - (ids == second).astype(F32)
+    incidence_t = incidence.T
     product = jnp.dot(incidence.astype(BF16), incidence_t.astype(BF16), preferred_element_type=F32)
     row = lax.broadcasted_iota(jnp.int32, (dates, dates), 0)
     col = lax.broadcasted_iota(jnp.int32, (dates, dates), 1)
@@ -53,7 +53,8 @@
         inverse = inverse + jnp.dot(inverse, power, precision=HIGHEST, preferred_element_type=F32)
         terms *= 2
     combos = LAGS * dates
-    key = first + dates * (second - first - 1)
+    key = (first + dates * (second - first - 1)).astype(F32)
+    key = jnp.broadcast_to(key, (8, pair_total)).T[:, 0:1].astype(jnp.int32)
     combo = lax.broadcasted_iota(jnp.int32, (pair_total, combos), 1)
     count = jnp.sum((combo == key).astype(F32), axis=0, keepdims=True)
     combo = lax.broadcasted_iota(jnp.int32, (dates, combos), 1)
@@ -102,14 +103,16 @@
 
 def kernel(
     n, slc, look_weight, pairs, series,
-    local, images, rim_parts, rim_send, rim_recv, weight, weights, planes, rim_planes,
+    local, packed, images, rim_parts, rim_send, rim_recv, weight, weights, planes, rim_planes,
     high, low, rim_high, rim_low, powers, solved, mine, slots, trend,
     send_sem, recv_sem, own_sem,
 ):
     band = lax.axis_index("band")
     me = lax.axis_index("gx")
     date_dev, _, rows, cols = slc.shape
-    halves, dates, _, block, strip = images.shape
+    chunks, dates, block, strip = images.shape
+    halves = chunks // 2
+    part_rows = block // 2
     pitch = dates + 8
     groups = date_dev * 2 * halves
 
@@ -127,23 +130,33 @@
         copy.start()
     own_tiles = [
         pltpu.make_async_copy(
-            slc.at[:, :, pl.ds(h * block, block), columns_of(me)],
-            images.at[h, pl.ds(me * date_dev, date_dev)],
-            own_sem.at[4 + h],
+            packed.at[c, :, :, columns_of(me)],
+            images.at[c, pl.ds(me * date_dev, date_dev)],
+            own_sem.at[4 + c],
         )
-        for h in range(halves)
+        for c in range(chunks)
     ]
-    for copy in own_tiles:
-        copy.start()
+
+    def pack(half):
+        for d in range(date_dev):
+            real = local[d, 0, half * block : half * block + block, :].astype(F32)
+            imag = local[d, 1, half * block : half * block + block, :].astype(F32)
+            for e in range(2):
+                at = slice(e * part_rows, (e + 1) * part_rows)
+                tile = jnp.concatenate([real[at], imag[at]], axis=0)
+                packed[2 * half + e, d] = tile.astype(BF16)
+
+    fetch.wait()
+    pack(0)
     greet_all(n, band, me)
 
-    def tile_copy(h, k, source):
+    def tile_copy(c, k, source):
         peer = lax.rem(me + k, n)
         return pltpu.make_async_remote_copy(
-            src_ref=slc.at[:, :, pl.ds(h * block, block), columns_of(peer)],
-            dst_ref=images.at[h, pl.ds(source * date_dev, date_dev)],
-            send_sem=send_sem.at[h, k],
-            recv_sem=recv_sem.at[h, k],
+            src_ref=packed.at[c, :, :, columns_of(peer)],
+            dst_ref=images.at[c, pl.ds(source * date_dev, date_dev)],
+            send_sem=send_sem.at[c, k],
+            recv_sem=recv_sem.at[c, k],
             device_id=(band, peer),
             device_id_type=MESH,
         )
@@ -153,8 +166,8 @@
         return pltpu.make_async_remote_copy(
             src_ref=rim_send.at[peer],
             dst_ref=rim_recv.at[source],
-            send_sem=send_sem.at[halves, k],
-            recv_sem=recv_sem.at[halves, k],
+            send_sem=send_sem.at[chunks, k],
+            recv_sem=recv_sem.at[chunks, k],
             device_id=(band, peer),
             device_id_type=MESH,
         )
@@ -163,8 +176,8 @@
         return pltpu.make_async_remote_copy(
             src_ref=mine,
             dst_ref=slots.at[source],
-            send_sem=send_sem.at[halves + 1, k],
-            recv_sem=recv_sem.at[halves + 1, k],
+            send_sem=send_sem.at[chunks + 1, k],
+            recv_sem=recv_sem.at[chunks + 1, k],
             device_id=(band, lax.rem(me + k, n)),
             device_id_type=MESH,
         )
@@ -209,7 +222,6 @@
     empty = jnp.zeros((groups, 256), F32)
     rim_parts[0] = empty
     rim_parts[n + 1] = empty
-    fetch.wait()
 
     def pick_rims(j, carry):
         slab = local[:, :, :, columns_of(j)].reshape(tall, strip)
@@ -225,11 +237,15 @@
 
     lax.fori_loop(0, n, join_rims, 0)
     start_all(rim_copy)
-    for half in range(1, halves):
-        start_all(functools.partial(tile_copy, half))
+    for c in range(1, chunks):
+        if c % 2 == 0:
+            pack(c // 2)
+        start_all(functools.partial(tile_copy, c))
+    for copy in own_tiles:
+        copy.start()
     rim_recv[me] = rim_send[me]
 
-    weights[...] = network_weights(pairs[...], dates, 2.0 * (pairs.shape[0] // n))
+    weights[...] = network_weights(pairs[...], dates, 2.0 * (pairs.shape[1] // n))
     w_high, w_low = split(weights[...])
     mix = jnp.concatenate([w_high, w_low], axis=0)
     column_ids = me * strip + lax.broadcasted_iota(jnp.int32, (1, strip), 1)
@@ -250,19 +266,19 @@
     for slot in range(powers.shape[0]):
         powers[slot, dates:pitch, :] = zero
 
-    def place_half(half):
+    def place_chunk(chunk):
+        row = chunk * part_rows
+
         def place(t, carry):
+            tile = images[chunk, t].astype(F32)
             for part in range(2):
-                plane = images[half, t, part].astype(F32)
-                heavy = plane * weight[1, half * block : half * block + block, :]
-                for q in range(block // 8):
-                    row = half * block + q * 8
-                    target = pl.ds(row * pitch + t, 8, stride=pitch)
-                    planes[part, target, :] = plane[q * 8 : q * 8 + 8]
-                    planes[part + 2, target, :] = heavy[q * 8 : q * 8 + 8]
+                plane = tile[part * part_rows : (part + 1) * part_rows]
+                target = pl.ds(row * pitch + t, part_rows, stride=pitch)
+                planes[part, target, :] = plane
+                planes[part + 2, target, :] = plane * weight[1, row : row + part_rows, :]
             return carry
 
-        lax.fori_loop(0, dates, place, 0, unroll=4)
+        lax.fori_loop(0, dates, place, 0, unroll=8)
 
     k = lax.broadcasted_iota(jnp.int32, (strip, strip), 0)
     c = lax.broadcasted_iota(jnp.int32, (strip, strip), 1)
@@ -337,7 +353,7 @@
 
     finish_all(functools.partial(tile_copy, 0))
     own_tiles[0].wait()
-    place_half(0)
+    place_chunk(0)
     finish_all(rim_copy)
 
     a = lax.broadcasted_iota(jnp.int32, (rows, 128), 0)
@@ -376,13 +392,16 @@
         rim_low[half] = l[:, half * 128 : half * 128 + 128]
 
     total = jnp.zeros((dates, strip), F32)
-    ready = block - RIM
-    total = stage(0, block, 0, ready, total)
-    for half in range(1, halves):
-        finish_all(functools.partial(tile_copy, half))
-        own_tiles[half].wait()
-        place_half(half)
-    total = stage(ready - RIM, rows, ready, rows, total)
+    done = 0
+    for c in range(chunks):
+        if c > 0:
+            finish_all(functools.partial(tile_copy, c))
+            own_tiles[c].wait()
+            place_chunk(c)
+        arrived = (c + 1) * part_rows
+        ready = rows if c == chunks - 1 else arrived - RIM
+        total = stage(max(done - RIM, 0), arrived, done, ready, total)
+        done = ready
 
     mean = jnp.sum(total, axis=1, keepdims=True)
     slope = jnp.sum(total * columns, axis=1, keepdims=True)
@@ -418,7 +437,8 @@
     pitch = dates + 8
     halves = rows // block
     planned = (LAGS + 1) * dates
-    most = rows - block + RIM
+    chunks = 2 * halves
+    most = block // 2 + RIM
     lines = 2 * halves * date_dev
 
     vmem = pl.BlockSpec(memory_space=pltpu.VMEM)
@@ -431,7 +451,8 @@
         out_specs=vmem,
         scratch_shapes=[
             pltpu.VMEM(slc_tiles.shape, BF16),
-            pltpu.VMEM((halves, dates, 2, block, strip), BF16),
+            pltpu.VMEM((chunks, date_dev, block, cols), BF16),
+            pltpu.VMEM((chunks, dates, block, strip), BF16),
             pltpu.VMEM((n + 2, lines, 256), F32),
             pltpu.VMEM((n, lines, 128), BF16),
             pltpu.VMEM((n, lines, 128), BF16),
@@ -448,14 +469,14 @@
             pltpu.VMEM((8, dates), F32),
             pltpu.VMEM((n, 8, dates), F32),
             pltpu.VMEM((dates, strip), F32),
-            dma((halves + 2, n)),
-            dma((halves + 2, n)),
-            dma((4 + halves,)),
+            dma((chunks + 2, n)),
+            dma((chunks + 2, n)),
+            dma((4 + chunks,)),
         ],
         compiler_params=pltpu.CompilerParams(
             collective_id=0, has_side_effects=True, vmem_limit_bytes=60 * MIB
         ),
-    )(slc_tiles, look_weight, pair_list)
+    )(slc_tiles, look_weight, pair_list.T)
 
 
 def solution(mesh):

time: 49.2 us -> 47.5 us (0.965)
  local copies, waits for them, and re-layouts: 3.71 us -> 2.26 us
    unnamed x2 -> x1, local copies, waits for them, and re-layouts: 3.71 us -> 2.26 us
where the time goes in v3:
time: 47.5 us; the launch traced here: 47.3 us
  Pallas kernels  45 us (95%)
  local copies, waits for them, and re-layouts  2.26 us (5%)
    pallas_call x1, Pallas kernels, body(): pl.pallas_call(functools.partial(kernel, n), out_shape=jax.ShapeDtypeStru...  45 us
    unnamed x1, local copies, waits for them, and re-layouts  2.26 us

profile of v3, /device:TPU:0, one launch (start us, length us, event | category | flops | bytes accessed | tf_op | source)
XLA Modules:
  0.0 47.3 jit_solution(18021852493748564754)
XLA Ops:
  0.0 45.0 %shard_map.37 = f32[64,32,128]{2,1,0:T(8,128)} custom-call(bf16[4,2,32,2048]{3,2,1,0:T(8,128)(2,1)} %slc.1, f32[32,2048]{1,0:T(8,128)} %look_weight.1, s32[2,192]{1,0:T(2,128)} %bitcast.1), custom_call_target="tpu_custom_call" | custom-call | tf_op jit(solution)/shard_map/pallas_call | solution.py:447
  45.0 2.3 %copy.5 = f32[64,32,128]{2,1,0:T(8,128)} copy(f32[64,32,128]{2,1,0:T(8,128)} %shard_map.37) | data formatting | bytes 2097152

commit v4 on v3

--- a/solution.py
+++ b/solution.py
@@ -28,6 +28,20 @@
 
     lax.fori_loop(1, n, greet, 0)
     pl.semaphore_wait(barrier, n - 1)
+
+
+def split(values):
+    high = values.astype(BF16)
+    low = (values - high.astype(F32)).astype(BF16)
+    return high, low
+
+
+def dot_split(a, b):
+    a_high, a_low = split(a)
+    b_high, b_low = split(b)
+    total = jnp.dot(a_high, b_high, preferred_element_type=F32)
+    total = total + jnp.dot(a_high, b_low, preferred_element_type=F32)
+    return total + jnp.dot(a_low, b_high, preferred_element_type=F32)
 
 
 def network_weights(pairs, dates, degree_bound):
@@ -49,9 +63,11 @@
     terms = 2
     need = 18.5 * (top + 1.0) / 2.0
     while terms < need:
-        power = jnp.dot(power, power, precision=HIGHEST, preferred_element_type=F32)
-        inverse = inverse + jnp.dot(inverse, power, precision=HIGHEST, preferred_element_type=F32)
+        power = dot_split(power, power)
+        inverse = inverse + dot_split(inverse, power)
         terms *= 2
+    rest = eye - jnp.dot(normal, inverse, precision=HIGHEST, preferred_element_type=F32)
+    inverse = inverse + jnp.dot(inverse, rest, precision=HIGHEST, preferred_element_type=F32)
     combos = LAGS * dates
     key = (first + dates * (second - first - 1)).astype(F32)
     key = jnp.broadcast_to(key, (8, pair_total)).T[:, 0:1].astype(jnp.int32)
@@ -67,12 +83,6 @@
     return jnp.dot(inverse, spread, precision=HIGHEST, preferred_element_type=F32)
 
 
-def split(values):
-    high = values.astype(BF16)
-    low = (values - high.astype(F32)).astype(BF16)
-    return high, low
-
-
 def cross(planes, first, second, rows):
     first = pl.ds(first, rows)
     second = pl.ds(second, rows)
@@ -102,9 +112,9 @@
 
 
 def kernel(
-    n, slc, look_weight, pairs, series,
+    n, slc, look_weight, pairs, series, trend,
     local, packed, images, rim_parts, rim_send, rim_recv, weight, weights, planes, rim_planes,
-    high, low, rim_high, rim_low, powers, solved, mine, slots, trend,
+    high, low, rim_high, rim_low, powers, solved, mine, slots,
     send_sem, recv_sem, own_sem,
 ):
     band = lax.axis_index("band")
@@ -199,6 +209,7 @@
         lax.fori_loop(1, n, finish, 0)
 
     start_all(functools.partial(tile_copy, 0))
+    start_all(functools.partial(tile_copy, 1))
 
     a = lax.broadcasted_iota(jnp.int32, (strip, 256), 0)
     b = lax.broadcasted_iota(jnp.int32, (strip, 256), 1)
@@ -229,15 +240,15 @@
         rim_parts[j + 1] = jnp.dot(gather, spread.astype(BF16), preferred_element_type=F32)
         return carry
 
-    lax.fori_loop(0, n, pick_rims, 0)
+    lax.fori_loop(0, n, pick_rims, 0, unroll=4)
 
     def join_rims(j, carry):
         rim_send[j] = (rim_parts[j, :, 0:128] + rim_parts[j + 2, :, 128:256]).astype(BF16)
         return carry
 
-    lax.fori_loop(0, n, join_rims, 0)
+    lax.fori_loop(0, n, join_rims, 0, unroll=4)
     start_all(rim_copy)
-    for c in range(1, chunks):
+    for c in range(2, chunks):
         if c % 2 == 0:
             pack(c // 2)
         start_all(functools.partial(tile_copy, c))
@@ -393,11 +404,10 @@
 
     total = jnp.zeros((dates, strip), F32)
     done = 0
-    for c in range(chunks):
-        if c > 0:
-            finish_all(functools.partial(tile_copy, c))
-            own_tiles[c].wait()
-            place_chunk(c)
+    for c in range(1, chunks):
+        finish_all(functools.partial(tile_copy, c))
+        own_tiles[c].wait()
+        place_chunk(c)
         arrived = (c + 1) * part_rows
         ready = rows if c == chunks - 1 else arrived - RIM
         total = stage(max(done - RIM, 0), arrived, done, ready, total)
@@ -409,6 +419,14 @@
     mine[...] = jnp.where(lane == 0, mean, slope).T[0:8]
     start_all(sum_copy)
     slots[me] = mine[...]
+
+    def unplace(t, carry):
+        for q in range(rows // 8):
+            piece = solved[pl.ds(q * 8 * dates + t, 8, stride=dates), :]
+            series[t, q * 8 : q * 8 + 8, :] = piece
+        return carry
+
+    lax.fori_loop(0, dates, unplace, 0, unroll=8)
     all_cols = lax.broadcasted_iota(jnp.int32, (1, cols), 1)
     all_cols = (2.0 * all_cols.astype(F32) + 1.0) / cols - 1.0
     square_sum = jnp.sum(all_cols * all_cols, axis=1, keepdims=True)
@@ -418,14 +436,10 @@
     date_slope = sums[:, 1:2] / (rows * square_sum)
     trend[...] = date_mean + date_slope * columns
 
-    def unplace(t, carry):
-        gone = trend[pl.ds(t, 1), :]
-        for q in range(rows // 8):
-            piece = solved[pl.ds(q * 8 * dates + t, 8, stride=dates), :]
-            series[t, q * 8 : q * 8 + 8, :] = piece - gone
-        return carry
-
-    lax.fori_loop(0, dates, unplace, 0, unroll=8)
+
+def remove_kernel(series, trend, corrected):
+    for t in range(series.shape[0]):
+        corrected[t] = series[t] - trend[t : t + 1, :]
 
 
 def body(slc_tiles, look_weight, pair_list):
@@ -438,17 +452,20 @@
     halves = rows // block
     planned = (LAGS + 1) * dates
     chunks = 2 * halves
-    most = block // 2 + RIM
+    most = block - RIM
     lines = 2 * halves * date_dev
 
     vmem = pl.BlockSpec(memory_space=pltpu.VMEM)
     anywhere = pl.BlockSpec(memory_space=pl.ANY)
     dma = pltpu.SemaphoreType.DMA
-    return pl.pallas_call(
+    series, trend = pl.pallas_call(
         functools.partial(kernel, n),
-        out_shape=jax.ShapeDtypeStruct((dates, rows, strip), F32),
+        out_shape=(
+            jax.ShapeDtypeStruct((dates, rows, strip), F32),
+            jax.ShapeDtypeStruct((dates, strip), F32),
+        ),
         in_specs=[anywhere, anywhere, vmem],
-        out_specs=vmem,
+        out_specs=(vmem, vmem),
         scratch_shapes=[
             pltpu.VMEM(slc_tiles.shape, BF16),
             pltpu.VMEM((chunks, date_dev, block, cols), BF16),
@@ -468,7 +485,6 @@
             pltpu.VMEM((rows * dates, strip), F32),
             pltpu.VMEM((8, dates), F32),
             pltpu.VMEM((n, 8, dates), F32),
-            pltpu.VMEM((dates, strip), F32),
             dma((chunks + 2, n)),
             dma((chunks + 2, n)),
             dma((4 + chunks,)),
@@ -478,6 +494,16 @@
         ),
     )(slc_tiles, look_weight, pair_list.T)
 
+    part = min(dates, 16)
+    cube = pl.BlockSpec((part, rows, strip), lambda i: (i, 0, 0))
+    return pl.pallas_call(
+        remove_kernel,
+        grid=(dates // part,),
+        out_shape=jax.ShapeDtypeStruct((dates, rows, strip), F32),
+        in_specs=[cube, pl.BlockSpec((part, strip), lambda i: (i, 0))],
+        out_specs=cube,
+    )(series, trend)
+
 
 def solution(mesh):
     return jax.shard_map(

time: 47.5 us -> 47.8 us (level)
  Pallas kernels: 45 us -> 47.6 us
  local copies, waits for them, and re-layouts: 2.26 us -> 0 us
    pallas_call x1 -> x2, Pallas kernels: 45 us -> 47.6 us  [the longest x1 44.2 us: body(): pl.pallas_call(functools.partial(kernel, n), out_shape=(jax.ShapeDtypeStr...]
    unnamed x1 -> x0, local copies, waits for them, and re-layouts: 2.26 us -> none
where the time goes in v4:
time: 47.8 us; the launch traced here: 47.6 us
  Pallas kernels  47.6 us (100%)
    pallas_call x1, Pallas kernels, body(): pl.pallas_call(functools.partial(kernel, n), out_shape=(jax.ShapeDtypeStr...  44.2 us
    pallas_call x1, Pallas kernels, body(): pl.pallas_call(remove_kernel, grid=(dates // part,), out_shape=jax.ShapeD...  3.38 us

profile of v4, /device:TPU:0, one launch (start us, length us, event | category | flops | bytes accessed | tf_op | source)
XLA Modules:
  0.0 47.6 jit_solution(1495554161154844018)
XLA Ops:
  0.0 44.2 %shard_map.37 = (f32[64,32,128]{2,1,0:T(8,128)}, f32[64,128]{1,0:T(8,128)}) custom-call(bf16[4,2,32,2048]{3,2,1,0:T(8,128)(2,1)} %slc.1, f32[32,2048]{1,0:T(8,128)} %look_weight.1, s32[2,192]{1,0:T(2,128)} %bitcast.1), custom_call_target="tpu_custom_call" | custom-call | tf_op jit(solution)/shard_map/pallas_call | solution.py:461
  44.2 3.4 %shard_map.38 = f32[64,32,128]{2,1,0:T(8,128)} custom-call(f32[64,32,128]{2,1,0:T(8,128)} %get-tuple-element.7.series, f32[64,128]{1,0:T(8,128)} %get-tuple-element.8.trend), custom_call_target="tpu_custom_call" | custom-call | tf_op jit(solution)/shard_map/pallas_call | solution.py:499

commit v5 on v4

--- a/solution.py
+++ b/solution.py
@@ -18,15 +18,19 @@
 MIB = 1024 * 1024
 
 
+def wrap(index, n):
+    return jnp.where(index >= n, index - n, index)
+
+
 def greet_all(n, band, me):
     barrier = pltpu.get_barrier_semaphore()
 
     def greet(k, carry):
-        peer = lax.rem(me + k, n)
+        peer = wrap(me + k, n)
         pl.semaphore_signal(barrier, inc=1, device_id=(band, peer), device_id_type=MESH)
         return carry
 
-    lax.fori_loop(1, n, greet, 0)
+    lax.fori_loop(1, n, greet, 0, unroll=True)
     pl.semaphore_wait(barrier, n - 1)
 
 
@@ -138,15 +142,6 @@
     ]
     for copy in weight_copies:
         copy.start()
-    own_tiles = [
-        pltpu.make_async_copy(
-            packed.at[c, :, :, columns_of(me)],
-            images.at[c, pl.ds(me * date_dev, date_dev)],
-            own_sem.at[4 + c],
-        )
-        for c in range(chunks)
-    ]
-
     def pack(half):
         for d in range(date_dev):
             real = local[d, 0, half * block : half * block + block, :].astype(F32)
@@ -160,56 +155,50 @@
     pack(0)
     greet_all(n, band, me)
 
-    def tile_copy(c, k, source):
-        peer = lax.rem(me + k, n)
-        return pltpu.make_async_remote_copy(
-            src_ref=packed.at[c, :, :, columns_of(peer)],
-            dst_ref=images.at[c, pl.ds(source * date_dev, date_dev)],
-            send_sem=send_sem.at[c, k],
-            recv_sem=recv_sem.at[c, k],
-            device_id=(band, peer),
-            device_id_type=MESH,
+    parts = [slice(0, 2)] + [slice(c, c + 1) for c in range(2, chunks)]
+    rim_at, sum_at = len(parts), len(parts) + 1
+
+    def tile_refs(part, peer):
+        size = part.stop - part.start
+        return (
+            packed.at[pl.ds(part.start, size), :, :, columns_of(peer)],
+            images.at[pl.ds(part.start, size), pl.ds(me * date_dev, date_dev)],
         )
 
-    def rim_copy(k, source):
-        peer = lax.rem(me + k, n)
-        return pltpu.make_async_remote_copy(
-            src_ref=rim_send.at[peer],
-            dst_ref=rim_recv.at[source],
-            send_sem=send_sem.at[chunks, k],
-            recv_sem=recv_sem.at[chunks, k],
-            device_id=(band, peer),
-            device_id_type=MESH,
-        )
-
-    def sum_copy(k, source):
-        return pltpu.make_async_remote_copy(
-            src_ref=mine,
-            dst_ref=slots.at[source],
-            send_sem=send_sem.at[chunks + 1, k],
-            recv_sem=recv_sem.at[chunks + 1, k],
-            device_id=(band, lax.rem(me + k, n)),
-            device_id_type=MESH,
-        )
-
-    def start_all(make):
+    def rim_refs(peer):
+        return rim_send.at[peer], rim_recv.at[me]
+
+    def sum_refs(peer):
+        return mine, slots.at[me]
+
+    def start_all(at, refs_of):
         def start(k, carry):
-            make(k, me).start()
+            peer = wrap(me + k, n)
+            source, target = refs_of(peer)
+            pltpu.make_async_remote_copy(
+                src_ref=source,
+                dst_ref=target,
+                send_sem=send_sem.at[at],
+                recv_sem=recv_sem.at[at],
+                device_id=(band, peer),
+                device_id_type=MESH,
+            ).start()
             return carry
 
-        lax.fori_loop(1, n, start, 0)
-
-    def finish_all(make):
-        def finish(k, carry):
-            one = make(k, lax.rem(me + n - k, n))
-            one.wait_send()
-            one.wait_recv()
-            return carry
-
-        lax.fori_loop(1, n, finish, 0)
-
-    start_all(functools.partial(tile_copy, 0))
-    start_all(functools.partial(tile_copy, 1))
+        lax.fori_loop(1, n, start, 0, unroll=5)
+        source, target = refs_of(me)
+        pltpu.make_async_copy(source, target, recv_sem.at[at]).start()
+
+    def start_tiles(at):
+        start_all(at, functools.partial(tile_refs, parts[at]))
+
+    def received(at, whole):
+        pltpu.make_async_copy(whole, whole, recv_sem.at[at]).wait()
+
+    def sent(at, others):
+        pltpu.make_async_copy(others, others, send_sem.at[at]).wait()
+
+    start_tiles(0)
 
     a = lax.broadcasted_iota(jnp.int32, (strip, 256), 0)
     b = lax.broadcasted_iota(jnp.int32, (strip, 256), 1)
@@ -247,14 +236,11 @@
         return carry
 
     lax.fori_loop(0, n, join_rims, 0, unroll=4)
-    start_all(rim_copy)
+    start_all(rim_at, rim_refs)
     for c in range(2, chunks):
         if c % 2 == 0:
             pack(c // 2)
-        start_all(functools.partial(tile_copy, c))
-    for copy in own_tiles:
-        copy.start()
-    rim_recv[me] = rim_send[me]
+        start_tiles(c - 1)
 
     weights[...] = network_weights(pairs[...], dates, 2.0 * (pairs.shape[1] // n))
     w_high, w_low = split(weights[...])
@@ -362,10 +348,10 @@
 
         return lax.fori_loop(0, (out_hi - out_lo) // together, some_rows, total)
 
-    finish_all(functools.partial(tile_copy, 0))
-    own_tiles[0].wait()
+    received(0, images.at[pl.ds(0, 2)])
     place_chunk(0)
-    finish_all(rim_copy)
+    place_chunk(1)
+    received(rim_at, rim_recv)
 
     a = lax.broadcasted_iota(jnp.int32, (rows, 128), 0)
     b = lax.broadcasted_iota(jnp.int32, (rows, 128), 1)
@@ -405,9 +391,9 @@
     total = jnp.zeros((dates, strip), F32)
     done = 0
     for c in range(1, chunks):
-        finish_all(functools.partial(tile_copy, c))
-        own_tiles[c].wait()
-        place_chunk(c)
+        if c > 1:
+            received(c - 1, images.at[pl.ds(c, 1)])
+            place_chunk(c)
         arrived = (c + 1) * part_rows
         ready = rows if c == chunks - 1 else arrived - RIM
         total = stage(max(done - RIM, 0), arrived, done, ready, total)
@@ -417,8 +403,7 @@
     slope = jnp.sum(total * columns, axis=1, keepdims=True)
     lane = lax.broadcasted_iota(jnp.int32, (dates, 128), 1)
     mine[...] = jnp.where(lane == 0, mean, slope).T[0:8]
-    start_all(sum_copy)
-    slots[me] = mine[...]
+    start_all(sum_at, sum_refs)
 
     def unplace(t, carry):
         for q in range(rows // 8):
@@ -430,16 +415,16 @@
     all_cols = lax.broadcasted_iota(jnp.int32, (1, cols), 1)
     all_cols = (2.0 * all_cols.astype(F32) + 1.0) / cols - 1.0
     square_sum = jnp.sum(all_cols * all_cols, axis=1, keepdims=True)
-    finish_all(sum_copy)
+    received(sum_at, slots)
+    others = pl.ds(0, (n - 1) * date_dev)
+    for at, part in enumerate(parts):
+        sent(at, images.at[pl.ds(part.start, part.stop - part.start), others])
+    sent(rim_at, rim_recv.at[pl.ds(0, n - 1)])
+    sent(sum_at, slots.at[pl.ds(0, n - 1)])
     sums = lax.fori_loop(1, n, lambda s, acc: acc + slots[s], slots[0]).T
     date_mean = sums[:, 0:1] / (rows * cols)
     date_slope = sums[:, 1:2] / (rows * square_sum)
     trend[...] = date_mean + date_slope * columns
-
-
-def remove_kernel(series, trend, corrected):
-    for t in range(series.shape[0]):
-        corrected[t] = series[t] - trend[t : t + 1, :]
 
 
 def body(slc_tiles, look_weight, pair_list):
@@ -485,24 +470,15 @@
             pltpu.VMEM((rows * dates, strip), F32),
             pltpu.VMEM((8, dates), F32),
             pltpu.VMEM((n, 8, dates), F32),
-            dma((chunks + 2, n)),
-            dma((chunks + 2, n)),
-            dma((4 + chunks,)),
+            dma((chunks + 1,)),
+            dma((chunks + 1,)),
+            dma((4,)),
         ],
         compiler_params=pltpu.CompilerParams(
             collective_id=0, has_side_effects=True, vmem_limit_bytes=60 * MIB
         ),
     )(slc_tiles, look_weight, pair_list.T)
-
-    part = min(dates, 16)
-    cube = pl.BlockSpec((part, rows, strip), lambda i: (i, 0, 0))
-    return pl.pallas_call(
-        remove_kernel,
-        grid=(dates // part,),
-        out_shape=jax.ShapeDtypeStruct((dates, rows, strip), F32),
-        in_specs=[cube, pl.BlockSpec((part, strip), lambda i: (i, 0))],
-        out_specs=cube,
-    )(series, trend)
+    return series - trend[:, None, :]
 
 
 def solution(mesh):

time: 47.8 us -> 44.9 us (0.939)
  Pallas kernels: 47.6 us -> 42.4 us
  other arithmetic: 0 us -> 2.34 us
    pallas_call x1 -> x0, Pallas kernels: 3.38 us -> none  [body(): pl.pallas_call(remove_kernel, grid=(dates // part,), out_shape=jax.ShapeD...]
    sub x0 -> x1, other arithmetic: none -> 2.34 us  [body(): return series - trend[:, None, :]]
    pallas_call x1, Pallas kernels: 44.2 us -> 42.4 us  [body(): pl.pallas_call(functools.partial(kernel, n), out_shape=(jax.ShapeDtypeStr...]
where the time goes in v5:
time: 44.9 us; the launch traced here: 44.8 us
  Pallas kernels  42.4 us (94%)
  other arithmetic  2.34 us (5%)
    pallas_call x1, Pallas kernels, body(): pl.pallas_call(functools.partial(kernel, n), out_shape=(jax.ShapeDtypeStr...  42.4 us
    sub x1, other arithmetic, body(): return series - trend[:, None, :]  2.34 us

profile of v5, /device:TPU:0, one launch (start us, length us, event | category | flops | bytes accessed | tf_op | source)
XLA Modules:
  0.0 44.8 jit_solution(851614225833441435)
XLA Ops:
  0.0 42.4 %shard_map.37 = (f32[64,32,128]{2,1,0:T(8,128)}, f32[64,128]{1,0:T(8,128)}) custom-call(bf16[4,2,32,2048]{3,2,1,0:T(8,128)(2,1)} %slc.1, f32[32,2048]{1,0:T(8,128)} %look_weight.1, s32[2,192]{1,0:T(2,128)} %bitcast.1), custom_call_target="tpu_custom_call" | custom-call | tf_op jit(solution)/shard_map/pallas_call | solution.py:446
  42.4 2.3 %broadcast_subtract_fusion = f32[64,32,128]{2,1,0:T(8,128)} fusion(f32[64,32,128]{2,1,0:T(8,128)} %get-tuple-element.7, f32[64,128]{1,0:T(8,128)} %get-tuple-element.8), kind=kLoop, calls=%fused_computation | loop fusion | flops 262144 | bytes 2129920 | tf_op jit(solution)/shard_map/sub | solution.py:481

commit v6 on v5

--- a/solution.py
+++ b/solution.py
@@ -31,7 +31,7 @@
         return carry
 
     lax.fori_loop(1, n, greet, 0, unroll=True)
-    pl.semaphore_wait(barrier, n - 1)
+    return barrier
 
 
 def split(values):
@@ -135,6 +135,7 @@
 
     fetch = pltpu.make_async_copy(slc, local, own_sem.at[0])
     fetch.start()
+    barrier = greet_all(n, band, me)
     sides = (lax.max(me - 1, 0), me, lax.min(me + 1, n - 1))
     weight_copies = [
         pltpu.make_async_copy(look_weight.at[:, columns_of(j)], weight.at[i], own_sem.at[1 + i])
@@ -153,7 +154,7 @@
 
     fetch.wait()
     pack(0)
-    greet_all(n, band, me)
+    pl.semaphore_wait(barrier, n - 1)
 
     parts = [slice(0, 2)] + [slice(c, c + 1) for c in range(2, chunks)]
     rim_at, sum_at = len(parts), len(parts) + 1
@@ -172,8 +173,9 @@
         return mine, slots.at[me]
 
     def start_all(at, refs_of):
-        def start(k, carry):
-            peer = wrap(me + k, n)
+        def start(i, carry):
+            k = i + n // 2 - 1
+            peer = wrap(me + jnp.where(k >= n, k - n + 1, k), n)
             source, target = refs_of(peer)
             pltpu.make_async_remote_copy(
                 src_ref=source,
@@ -315,15 +317,12 @@
                 half = lax.div(r, block)
                 side = jnp.where((k >> 3) == lax.rem(r, block), rim_near, 0.0).astype(BF16)
                 matrix = jnp.concatenate([main, side], axis=0)
-                looked = jnp.dot(
-                    jnp.concatenate([high[at], rim_high[half]], axis=1),
-                    matrix,
-                    preferred_element_type=F32,
-                ) + jnp.dot(
-                    jnp.concatenate([low[at], rim_low[half]], axis=1),
-                    matrix,
-                    preferred_element_type=F32,
+                left = jnp.concatenate([high[at], low[at]], axis=0)
+                right = jnp.concatenate([rim_high[half], rim_low[half]], axis=0)
+                halved = jnp.dot(
+                    jnp.concatenate([left, right], axis=1), matrix, preferred_element_type=F32
                 )
+                looked = halved[: (LAGS + 1) * dates] + halved[(LAGS + 1) * dates :]
                 powers[i, 0:dates, :] = looked[0:dates]
                 looks.append(looked)
             sines = []

time: 44.9 us -> 43.8 us (0.976)
  Pallas kernels: 42.4 us -> 41.3 us
    pallas_call x1, Pallas kernels: 42.4 us -> 41.3 us  [body(): pl.pallas_call(functools.partial(kernel, n), out_shape=(jax.ShapeDtypeStr...]
where the time goes in v6:
time: 43.8 us; the launch traced here: 43.6 us
  Pallas kernels  41.3 us (94%)
  other arithmetic  2.34 us (5%)
    pallas_call x1, Pallas kernels, body(): pl.pallas_call(functools.partial(kernel, n), out_shape=(jax.ShapeDtypeStr...  41.3 us
    sub x1, other arithmetic, body(): return series - trend[:, None, :]  2.34 us

profile of v6, /device:TPU:0, one launch (start us, length us, event | category | flops | bytes accessed | tf_op | source)
XLA Modules:
  0.0 43.6 jit_solution(8548821035667107891)
XLA Ops:
  0.0 41.3 %shard_map.37 = (f32[64,32,128]{2,1,0:T(8,128)}, f32[64,128]{1,0:T(8,128)}) custom-call(bf16[4,2,32,2048]{3,2,1,0:T(8,128)(2,1)} %slc.1, f32[32,2048]{1,0:T(8,128)} %look_weight.1, s32[2,192]{1,0:T(2,128)} %bitcast.1), custom_call_target="tpu_custom_call" | custom-call | tf_op jit(solution)/shard_map/pallas_call | solution.py:445
  41.3 2.3 %broadcast_subtract_fusion = f32[64,32,128]{2,1,0:T(8,128)} fusion(f32[64,32,128]{2,1,0:T(8,128)} %get-tuple-element.7, f32[64,128]{1,0:T(8,128)} %get-tuple-element.8), kind=kLoop, calls=%fused_computation | loop fusion | flops 262144 | bytes 2129920 | tf_op jit(solution)/shard_map/sub | solution.py:480

commit v7 on v6

--- a/solution.py
+++ b/solution.py
@@ -277,7 +277,7 @@
                 planes[part + 2, target, :] = plane * weight[1, row : row + part_rows, :]
             return carry
 
-        lax.fori_loop(0, dates, place, 0, unroll=8)
+        lax.fori_loop(0, dates, place, 0, unroll=16)
 
     k = lax.broadcasted_iota(jnp.int32, (strip, strip), 0)
     c = lax.broadcasted_iota(jnp.int32, (strip, strip), 1)
@@ -415,15 +415,15 @@
     all_cols = (2.0 * all_cols.astype(F32) + 1.0) / cols - 1.0
     square_sum = jnp.sum(all_cols * all_cols, axis=1, keepdims=True)
     received(sum_at, slots)
+    sums = lax.fori_loop(1, n, lambda s, acc: acc + slots[s], slots[0], unroll=True).T
+    date_mean = sums[:, 0:1] / (rows * cols)
+    date_slope = sums[:, 1:2] / (rows * square_sum)
+    trend[...] = date_mean + date_slope * columns
     others = pl.ds(0, (n - 1) * date_dev)
     for at, part in enumerate(parts):
         sent(at, images.at[pl.ds(part.start, part.stop - part.start), others])
     sent(rim_at, rim_recv.at[pl.ds(0, n - 1)])
     sent(sum_at, slots.at[pl.ds(0, n - 1)])
-    sums = lax.fori_loop(1, n, lambda s, acc: acc + slots[s], slots[0]).T
-    date_mean = sums[:, 0:1] / (rows * cols)
-    date_slope = sums[:, 1:2] / (rows * square_sum)
-    trend[...] = date_mean + date_slope * columns
 
 
 def body(slc_tiles, look_weight, pair_list):
@@ -459,14 +459,14 @@
             pltpu.VMEM((n, lines, 128), BF16),
             pltpu.VMEM((3, rows, strip), F32),
             pltpu.VMEM((dates, LAGS * dates), F32),
-            pltpu.VMEM((4, rows * pitch, strip), F32),
+            pltpu.VMEM((4, (rows + 1) * pitch, strip), F32),
             pltpu.VMEM((4, halves * pitch, 128), F32),
             pltpu.VMEM((most, planned, strip), BF16),
             pltpu.VMEM((most, planned, strip), BF16),
             pltpu.VMEM((halves, planned, 128), BF16),
             pltpu.VMEM((halves, planned, 128), BF16),
             pltpu.VMEM((4, pitch, strip), F32),
-            pltpu.VMEM((rows * dates, strip), F32),
+            pltpu.VMEM(((rows + 1) * dates, strip), F32),
             pltpu.VMEM((8, dates), F32),
             pltpu.VMEM((n, 8, dates), F32),
             dma((chunks + 1,)),

time: 43.8 us -> 43.9 us (level)
  no operation moved by 1% of the time
where the time goes in v7:
time: 43.9 us; the launch traced here: 43.7 us
  Pallas kernels  41.3 us (94%)
  other arithmetic  2.34 us (5%)
    pallas_call x1, Pallas kernels, body(): pl.pallas_call(functools.partial(kernel, n), out_shape=(jax.ShapeDtypeStr...  41.3 us
    sub x1, other arithmetic, body(): return series - trend[:, None, :]  2.34 us

profile of v7, /device:TPU:0, one launch (start us, length us, event | category | flops | bytes accessed | tf_op | source)
XLA Modules:
  0.0 43.7 jit_solution(9699065535156490190)
XLA Ops:
  0.0 41.3 %shard_map.37 = (f32[64,32,128]{2,1,0:T(8,128)}, f32[64,128]{1,0:T(8,128)}) custom-call(bf16[4,2,32,2048]{3,2,1,0:T(8,128)(2,1)} %slc.1, f32[32,2048]{1,0:T(8,128)} %look_weight.1, s32[2,192]{1,0:T(2,128)} %bitcast.1), custom_call_target="tpu_custom_call" | custom-call | tf_op jit(solution)/shard_map/pallas_call | solution.py:445
  41.3 2.3 %broadcast_subtract_fusion = f32[64,32,128]{2,1,0:T(8,128)} fusion(f32[64,32,128]{2,1,0:T(8,128)} %get-tuple-element.7, f32[64,128]{1,0:T(8,128)} %get-tuple-element.8), kind=kLoop, calls=%fused_computation | loop fusion | flops 262144 | bytes 2129920 | tf_op jit(solution)/shard_map/sub | solution.py:480
